TPU v7x, 32 devices: a whole 2x2x4 slice. The times are simulated.
32 devices in a mesh: win: 4 (over y, x), seq: 8 (over z, core).
Axes of the slice: x: 2, y: 2, z: 4, core: 2. Of those that a mesh axis runs over, the one named last changes fastest.
Arguments:
- tokens: bfloat16 [16, 2048, 1024], P('win', 'seq'), may hold values from -6 to 6
- condition: bfloat16 [16, 2048, 1024], P('win', 'seq'), may hold values from -4 to 4
- valid_mask: int32 [16, 2048], P('win', 'seq'), may hold values from 0 to 1, as said below
- w_qkv: bfloat16 [1024, 3072], P(('win', 'seq')), may hold values from -0.1875 to 0.1875
- w_out: bfloat16 [1024, 1024], P(('win', 'seq')), may hold values from -1.5 to 1.5
- w_fc: bfloat16 [1024, 4096], P(('win', 'seq')), may hold values from -0.1875 to 0.1875
- w_down: bfloat16 [4096, 1024], P(('win', 'seq')), may hold values from -0.09375 to 0.09375
- norm_gains: bfloat16 [2, 1024], P(None, ('win', 'seq')), may hold values from 0.099609375 to 1.8984375
- biases: bfloat16 [6, 1024], P(None, ('win', 'seq')), may hold values from -2 to 2
- fc_bias: bfloat16 [4096], P(('win', 'seq')), may hold values from -2 to 2
- cotangent: bfloat16 [16, 2048, 1024], P('win', 'seq'), may hold values from -6 to 6
Outputs:
- output: bfloat16 [16, 2048, 1024], P('win', 'seq')
- grad_input: bfloat16 [16, 2048, 1024], P('win', 'seq')
- grad_w_qkv: float32 [1024, 3072], P(('win', 'seq'))
- grad_w_out: float32 [1024, 1024], P(('win', 'seq'))
- grad_w_fc: float32 [1024, 4096], P(('win', 'seq'))
- grad_w_down: float32 [4096, 1024], P(('win', 'seq'))
- grad_gains: float32 [2, 1024], P(None, ('win', 'seq'))
- grad_biases: float32 [6, 1024], P(None, ('win', 'seq'))
- grad_fc_bias: float32 [4096], P(('win', 'seq'))
Inputs may be any that keep to these rules, and one draw needn't show every extreme that they name: `valid_mask`: in each window the positions with 1 come first and those with 0 after them; in each aligned group of 4 windows one window is all ones.
All inputs are finite; a program needn't handle non-finite values.
Results may differ from a plain program's by a relative error of at most 0.012.
Values may be sent and summed in bfloat16 or wider, within the bound.
A program may use at most 256 MiB of HBM per device.

v0:
```python
from functools import partial

import jax
import jax.numpy as jnp
from jax import lax
from jax.sharding import PartitionSpec as P

HEADS = 16
BLOCK = 128


def layer_norm(rows_in, gain_vec, shift_vec):
    row_mean = jnp.mean(rows_in, axis=-1, keepdims=True)
    centered = rows_in - row_mean
    row_var = jnp.mean(centered * centered, axis=-1, keepdims=True)
    return centered * lax.rsqrt(row_var + 1e-05) * gain_vec + shift_vec


def outer_sum(first, second):
    return lax.dot_general(
        first, second, (((0,), (0,)), ((), ())), preferred_element_type=jnp.float32
    )


def times_transposed(first, second):
    return lax.dot_general(
        first, second, (((1,), (1,)), ((), ())), preferred_element_type=jnp.float32
    )


def masked_scores(queries_h, keys_h):
    scores = (
        jnp.einsum("bqhd,bkhd->bhqk", queries_h, keys_h, preferred_element_type=jnp.float32) * 0.125
    )
    causal = lax.broadcasted_iota(jnp.int32, scores.shape, 2) >= lax.broadcasted_iota(
        jnp.int32, scores.shape, 3
    )
    return jnp.where(causal, scores, -1e30)


def body(
    tokens,
    condition,
    valid_mask,
    w_qkv,
    w_out,
    w_fc,
    w_down,
    norm_gains,
    biases,
    fc_bias,
    cotangent,
):
    window_count, span_rows, model_width = tokens.shape
    row_total = window_count * span_rows
    head_size = model_width // HEADS
    head_shape = (row_total // BLOCK, BLOCK, HEADS, head_size)
    keep_rows = valid_mask.reshape(row_total, 1).astype(jnp.float32)
    hidden = tokens.reshape(row_total, model_width).astype(jnp.float32) + condition.reshape(
        row_total, model_width
    ).astype(jnp.float32)
    full_qkv, full_out, full_gains, full_biases = (
        lax.all_gather(w_qkv, ("win", "seq"), axis=0, tiled=True),
        lax.all_gather(w_out, ("win", "seq"), axis=0, tiled=True),
        lax.all_gather(norm_gains, ("win", "seq"), axis=1, tiled=True),
        lax.all_gather(biases, ("win", "seq"), axis=1, tiled=True),
    )
    gain_f = full_gains.astype(jnp.float32)
    bias_f = full_biases.astype(jnp.float32)
    normed_f, norm_back_one = jax.vjp(layer_norm, hidden, gain_f[0], bias_f[0])
    normed = normed_f.astype(jnp.bfloat16)
    projected = jnp.dot(normed, full_qkv, preferred_element_type=jnp.float32)
    queries = (projected[:, :model_width] + bias_f[1]).astype(jnp.bfloat16).reshape(head_shape)
    key_rows = projected[:, model_width : 2 * model_width].astype(jnp.bfloat16).reshape(head_shape)
    values = (projected[:, 2 * model_width :] + bias_f[2]).astype(jnp.bfloat16).reshape(head_shape)
    scores = masked_scores(queries, key_rows)
    row_max = jnp.max(scores, axis=-1, keepdims=True)
    log_total = row_max + jnp.log(jnp.sum(jnp.exp(scores - row_max), axis=-1, keepdims=True))
    probs = jnp.exp(scores - log_total).astype(jnp.bfloat16)
    mixed = jnp.einsum("bhqk,bkhd->bqhd", probs, values, preferred_element_type=jnp.float32)
    mixed = mixed.reshape(row_total, model_width).astype(jnp.bfloat16)
    after_attn = hidden + jnp.dot(mixed, full_out, preferred_element_type=jnp.float32) + bias_f[3]
    full_fc, full_down, full_fc_bias = (
        lax.all_gather(w_fc, ("win", "seq"), axis=0, tiled=True),
        lax.all_gather(w_down, ("win", "seq"), axis=0, tiled=True),
        lax.all_gather(fc_bias, ("win", "seq"), axis=0, tiled=True),
    )
    normed_two_f, norm_back_two = jax.vjp(layer_norm, after_attn, gain_f[1], bias_f[4])
    normed_two = normed_two_f.astype(jnp.bfloat16)
    pre_gelu = jnp.dot(
        normed_two, full_fc, preferred_element_type=jnp.float32
    ) + full_fc_bias.astype(jnp.float32)
    gelu_f, gelu_back = jax.vjp(partial(jax.nn.gelu, approximate=False), pre_gelu)
    gelu_out = gelu_f.astype(jnp.bfloat16)
    final_rows = (
        after_attn + jnp.dot(gelu_out, full_down, preferred_element_type=jnp.float32) + bias_f[5]
    )
    output = (final_rows * keep_rows).astype(jnp.bfloat16).reshape(tokens.shape)
    back_fc, back_down = (
        lax.all_gather(w_fc, ("win", "seq"), axis=0, tiled=True),
        lax.all_gather(w_down, ("win", "seq"), axis=0, tiled=True),
    )
    grad_final = cotangent.reshape(row_total, model_width).astype(jnp.float32) * keep_rows
    grad_mlp = grad_final.astype(jnp.bfloat16)
    grad_down_local = outer_sum(gelu_out, grad_mlp)
    grad_down_bias = jnp.sum(grad_mlp.astype(jnp.float32), axis=0)
    grad_gelu = times_transposed(grad_mlp, back_down)
    grad_pre = gelu_back(grad_gelu)[0].astype(jnp.bfloat16)
    grad_fc_local = outer_sum(normed_two, grad_pre)
    grad_fc_bias_local = jnp.sum(grad_pre.astype(jnp.float32), axis=0)
    grad_w_fc, grad_w_down, grad_fc_bias = (
        lax.psum_scatter(grad_fc_local, ("win", "seq"), scatter_dimension=0, tiled=True),
        lax.psum_scatter(grad_down_local, ("win", "seq"), scatter_dimension=0, tiled=True),
        lax.psum_scatter(grad_fc_bias_local, ("win", "seq"), scatter_dimension=0, tiled=True),
    )
    grad_normed_two = times_transposed(grad_pre, back_fc)
    grad_after_norm, grad_gain_two, grad_shift_two = norm_back_two(grad_normed_two)
    grad_after = grad_final + grad_after_norm
    back_qkv, back_out = (
        lax.all_gather(w_qkv, ("win", "seq"), axis=0, tiled=True),
        lax.all_gather(w_out, ("win", "seq"), axis=0, tiled=True),
    )
    grad_attn = grad_after.astype(jnp.bfloat16)
    grad_out_local = outer_sum(mixed, grad_attn)
    grad_out_bias = jnp.sum(grad_attn.astype(jnp.float32), axis=0)
    grad_mixed = times_transposed(grad_attn, back_out).astype(jnp.bfloat16).reshape(head_shape)
    probs_full = jnp.exp(masked_scores(queries, key_rows) - log_total)
    grad_probs = jnp.einsum(
        "bqhd,bkhd->bhqk", grad_mixed, values, preferred_element_type=jnp.float32
    )
    grad_values = jnp.einsum(
        "bhqk,bqhd->bkhd", probs, grad_mixed, preferred_element_type=jnp.float32
    )
    grad_values = grad_values.reshape(row_total, model_width).astype(jnp.bfloat16)
    grad_scores = probs_full * (
        grad_probs - jnp.sum(probs_full * grad_probs, axis=-1, keepdims=True)
    )
    grad_scores = grad_scores.astype(jnp.bfloat16)
    grad_queries = (
        jnp.einsum("bhqk,bkhd->bqhd", grad_scores, key_rows, preferred_element_type=jnp.float32)
        * 0.125
    )
    grad_keys = (
        jnp.einsum("bhqk,bqhd->bkhd", grad_scores, queries, preferred_element_type=jnp.float32)
        * 0.125
    )
    grad_queries = grad_queries.reshape(row_total, model_width).astype(jnp.bfloat16)
    grad_keys = grad_keys.reshape(row_total, model_width).astype(jnp.bfloat16)
    grad_query_bias = jnp.sum(grad_queries.astype(jnp.float32), axis=0)
    grad_value_bias = jnp.sum(grad_values.astype(jnp.float32), axis=0)
    grad_projected = jnp.concatenate([grad_queries, grad_keys, grad_values], axis=1)
    grad_qkv_local = outer_sum(normed, grad_projected)
    grad_normed = times_transposed(grad_projected, back_qkv)
    grad_hidden_norm, grad_gain_one, grad_shift_one = norm_back_one(grad_normed)
    grad_input = (grad_after + grad_hidden_norm).astype(jnp.bfloat16).reshape(tokens.shape)
    gains_local = jnp.stack([grad_gain_one, grad_gain_two])
    biases_local = jnp.stack(
        [
            grad_shift_one,
            grad_query_bias,
            grad_value_bias,
            grad_out_bias,
            grad_shift_two,
            grad_down_bias,
        ]
    )
    grad_w_qkv, grad_w_out, grad_gains, grad_biases = (
        lax.psum_scatter(grad_qkv_local, ("win", "seq"), scatter_dimension=0, tiled=True),
        lax.psum_scatter(grad_out_local, ("win", "seq"), scatter_dimension=0, tiled=True),
        lax.psum_scatter(gains_local, ("win", "seq"), scatter_dimension=1, tiled=True),
        lax.psum_scatter(biases_local, ("win", "seq"), scatter_dimension=1, tiled=True),
    )
    return (
        output,
        grad_input,
        grad_w_qkv,
        grad_w_out,
        grad_w_fc,
        grad_w_down,
        grad_gains,
        grad_biases,
        grad_fc_bias,
    )


def solution(mesh):
    return jax.shard_map(
        body,
        mesh=mesh,
        in_specs=(
            P("win", "seq", None),
            P("win", "seq", None),
            P("win", "seq"),
            P(("win", "seq"), None),
            P(("win", "seq"), None),
            P(("win", "seq"), None),
            P(("win", "seq"), None),
            P(None, ("win", "seq")),
            P(None, ("win", "seq")),
            P(("win", "seq")),
            P("win", "seq", None),
        ),
        out_specs=(
            P("win", "seq", None),
            P("win", "seq", None),
            P(("win", "seq"), None),
            P(("win", "seq"), None),
            P(("win", "seq"), None),
            P(("win", "seq"), None),
            P(None, ("win", "seq")),
            P(None, ("win", "seq")),
            P(("win", "seq")),
        ),
        check_vma=False,
    )
```

profile of v0, /device:TPU:0, one launch (start us, length us, event | category | flops | bytes accessed | tf_op | source)
XLA Modules:
  0.0 1377.7 jit_solution(3308283979003300578)
XLA Ops:
  13.5 43.1 %all-gather = bf16[32,32,2]{1,2,0:T(2,128)(2,1)S(1)} all-gather(bf16[1,32,2]{1,2,0:T(2,128)(2,1)S(1)} %bitcast.185), channel_id=1, replica_groups=mesh['win'=4,'seq'=8] {'win','seq'}, dimensions={0}, use_global_device_ids=true | all-gather | bytes 4224 | tf_op jit(solution)/shard_map/all_gather | solution.py:65
  56.7 36.6 %all-gather.2 = bf16[32,1,128]{2,1,0:T(2,128)(2,1)S(1)} all-gather(bf16[1,1,128]{2,1,0:T(2,128)(2,1)S(1)} %bitcast.186), channel_id=1, replica_groups=mesh['win'=4,'seq'=8] {'win','seq'}, dimensions={0}, use_global_device_ids=true | all-gather | bytes 8448 | tf_op jit(solution)/shard_map/all_gather | solution.py:86
  93.3 38.7 %all-gather.1 = bf16[32,32,6]{1,2,0:T(8,128)(2,1)S(1)} all-gather(bf16[1,32,6]{1,2,0:T(8,128)(2,1)S(1)} %bitcast.184), channel_id=1, replica_groups=mesh['win'=4,'seq'=8] {'win','seq'}, dimensions={0}, use_global_device_ids=true | all-gather | bytes 12672 | tf_op jit(solution)/shard_map/all_gather | solution.py:66
  141.0 8.7 fusion.37
  153.3 6.4 reshape.193
  205.5 15.0 %all-gather.12.cloned.1.call-done = bf16[1024,4096]{1,0:T(8,128)(2,1)} async-done(((bf16[32,4096]{1,0:T(8,128)(2,1)}), bf16[1024,4096]{1,0:T(8,128)(2,1)}) %all-gather.12.cloned.1.call-update) | async-done | bytes 8388624 | tf_op jit(solution)/shard_map/all_gather | solution.py:84
  220.5 17.2 %fusion.27 = f32[1024,4096]{1,0:T(8,128)} fusion(bf16[1024,4096]{1,0:T(8,128)(2,1)} %all-gather.12.cloned.1.call-done, f32[1024,1024]{1,0:T(8,128)} %copy-done.10, f32[1024]{0:T(1024)S(1)} %bitcast.179, f32[1024]{0:T(1024)S(1)} %bitcast.170, f32[1024]{0:T(1024)S(1)} %fusion.23, f32[1024]{0:T(1024)S(1)} %broadcast_multiply_fusion), kind=kOutput, calls=%fused_computation.87 | convolution fusion | flops 8595177472 | bytes 29376512 | tf_op jit(solution)/shard_map/dot_general | solution.py:90
  237.8 61.5 %all-gather.14.cloned.1.call-done = bf16[4096,1024]{1,0:T(8,128)(2,1)} async-done(((bf16[128,1024]{1,0:T(8,128)(2,1)}), bf16[4096,1024]{1,0:T(8,128)(2,1)}) %all-gather.14.cloned.1.call-update) | async-done | bytes 8388624 | tf_op jit(solution)/shard_map/all_gather | solution.py:85
  299.3 52.0 %convert_reduce_fusion = (f32[4096]{0:T(1024)}, bf16[1024,4096]{1,0:T(8,128)(2,1)}, f32[1024,4096]{1,0:T(8,128)}) fusion(f32[1024,4096]{1,0:T(8,128)} %fusion.27, f32[4096]{0:T(1024)S(1)} %bitcast.154, bf16[1024,1024]{1,0:T(8,128)(2,1)S(1)} %copy-done.20, bf16[4096,1024]{1,0:T(8,128)(2,1)} %all-gather.14.cloned.1.call-done), kind=kOutput, calls=%fused_computation.2 | convolution fusion | flops 8904503296 | bytes 52461568 | tf_op jit(solution)/shard_map/dot_general | solution.py:26
  351.3 14.9 %multiply_reduce_fusion.1 = (f32[1024]{0:T(1024)S(1)}, f32[1024]{0:T(1024)S(1)}, f32[1024]{0:T(1024)S(1)}, f32[1024,1024]{1,0:T(8,128)S(1)}) fusion(f32[1024,1024]{1,0:T(8,128)S(1)} %copy-done.11, f32[1024]{0:T(1024)S(1)} %copy-done.42, f32[1024]{0:T(1024)S(1)} %copy-done.37, f32[1024]{0:T(1024)S(1)} %bitcast.171, ...), kind=kOutput, calls=%fused_computation.41 | convolution fusion | flops 8598320128 | bytes 25190400 | tf_op jit(solution)/shard_map/dot_general | solution.py:26
  387.6 8.5 convert_reduce_fusion.3
  417.7 10.1 multiply_reduce_fusion.2
  430.7 6.5 fusion.12
  437.3 12.2 fusion.38
  450.2 16.9 %fusion.26 = f32[1024,4096]{1,0:T(8,128)} fusion(bf16[1024,4096]{1,0:T(8,128)(2,1)} %get-tuple-element.16, f32[1024,1024]{1,0:T(8,128)} %copy-done.10, f32[1024]{0:T(1024)S(1)} %bitcast.180, f32[1024]{0:T(1024)S(1)} %bitcast.173, f32[1024]{0:T(1024)S(1)} %copy-done.42, f32[1024]{0:T(1024)S(1)} %copy-done.37), kind=kOutput, calls=%fused_computation.86 | convolution fusion | flops 8595177472 | bytes 29376512 | tf_op jit(solution)/shard_map/dot_general | solution.py:20
  467.2 12.3 multiply_convert_fusion
  482.7 11.5 fusion.39
  494.9 39.7 %all-reduce = f32[4096]{0:T(1024)S(1)} all-reduce(f32[4096]{0:T(1024)S(1)} %copy-done.45), channel_id=8, replica_groups=mesh['win'=4,'seq'=8] {'win','seq'}, use_global_device_ids=true, to_apply=%region_26.27.clone | all-reduce | flops 4096 | bytes 32768
  544.6 12.2 multiply_convert_fusion.5
  562.9 131.4 %reduce-scatter.21.cloned.1.call-done = f32[32,6]{1,0:T(8,128)} async-done(((f32[1024,6]{1,0:T(8,128)}), f32[32,6]{1,0:T(8,128)}) %reduce-scatter.21.cloned.1.call-update) | async-done | bytes 784
  695.6 140.1 %reduce-scatter.13.cloned.1.call-done = f32[32,1024]{1,0:T(8,128)} async-done(((f32[1024,1024]{1,0:T(8,128)}), f32[32,1024]{1,0:T(8,128)}) %reduce-scatter.13.cloned.1.call-update) | async-done | bytes 131088 | tf_op jit(solution)/shard_map/reduce_scatter | solution.py:169
  835.8 158.9 %reduce-scatter.11.cloned.1.call-done = f32[32,3072]{1,0:T(8,128)} async-done(((f32[1024,3072]{1,0:T(8,128)}), f32[32,3072]{1,0:T(8,128)}) %reduce-scatter.11.cloned.1.call-update) | async-done | bytes 393232 | tf_op jit(solution)/shard_map/reduce_scatter | solution.py:168
  994.7 188.7 %reduce-scatter.15.cloned.1.call-done = f32[32,4096]{1,0:T(8,128)} async-done(((f32[1024,4096]{1,0:T(8,128)}), f32[32,4096]{1,0:T(8,128)}) %reduce-scatter.15.cloned.1.call-update) | async-done | bytes 524304 | tf_op jit(solution)/shard_map/reduce_scatter | solution.py:112
  1183.4 187.2 %reduce-scatter.17.cloned.1.call-done = f32[128,1024]{1,0:T(8,128)} async-done(((f32[4096,1024]{1,0:T(8,128)}), f32[128,1024]{1,0:T(8,128)}) %reduce-scatter.17.cloned.1.call-update) | async-done | bytes 524304 | tf_op jit(solution)/shard_map/reduce_scatter | solution.py:113
  (211 shorter events, 132.1 us)
Async XLA Ops:
  7.2 49.5 %copy-start.52 = (bf16[128]{0:T(256)(128)(2,1)S(1)}, bf16[128]{0:T(256)(128)(2,1)}, u32[]{:S(2)}) copy-start(bf16[128]{0:T(256)(128)(2,1)} %param.20) | copy-start | bytes 772
  7.2 86.1 %copy-start.50 = (bf16[6,32]{1,0:T(8,128)(2,1)S(1)}, bf16[6,32]{1,0:T(8,128)(2,1)}, u32[]{:S(2)}) copy-start(bf16[6,32]{1,0:T(8,128)(2,1)} %param.19) | copy-start | bytes 1156
  7.2 132.5 %all-gather.8.cloned.1.call-start = ((), (), s32[]{:S(2)}) async-start(), calls=%async_computation.6 | async-start | bytes 6488064 | tf_op jit(solution)/shard_map/all_gather | solution.py:63
  8.0 188.6 %all-gather.10.cloned.1.call-start = ((), (), s32[]{:S(2)}) async-start(), calls=%async_computation.7 | async-start | bytes 2162688 | tf_op jit(solution)/shard_map/all_gather | solution.py:64
  8.7 211.8 %all-gather.12.cloned.1.call-start = ((), (), s32[]{:S(2)}) async-start(), calls=%async_computation.8 | async-start | bytes 8650752 | tf_op jit(solution)/shard_map/all_gather | solution.py:84
  9.4 289.8 %all-gather.14.cloned.1.call-start = ((), (), s32[]{:S(2)}) async-start(), calls=%async_computation.9 | async-start | bytes 8650752 | tf_op jit(solution)/shard_map/all_gather | solution.py:85
  10.0 551.5 %reduce-scatter.19.cloned.1.call-start = ((), (), s32[]{:S(2)}) async-start(), calls=%async_computation.14 | async-start | bytes 540672
  12.9 126.0 %copy-start.28 = (f32[1,2,4,128]{3,1,2,0:T(2,128)}, f32[1,2,4,128]{3,1,2,0:T(2,128)S(1)}, u32[]{:S(2)}) copy-start(f32[1,2,4,128]{3,1,2,0:T(2,128)S(1)} %copy.114) | copy-start | bytes 12292
  13.5 123.6 %copy-start.26 = (f32[1,2,4,128]{3,1,2,0:T(2,128)}, f32[1,2,4,128]{3,1,2,0:T(2,128)S(1)}, u32[]{:S(2)}) copy-start(f32[1,2,4,128]{3,1,2,0:T(2,128)S(1)} %copy.117) | copy-start | bytes 12292
  136.1 84.4 %copy-start.43 = (f32[1,1024]{1,0:T(1,128)}, f32[1,1024]{1,0:T(1,128)S(1)}, u32[]{:S(2)}) copy-start(f32[1,1024]{1,0:T(1,128)S(1)} %get-tuple-element.34) | copy-start | bytes 12292
  137.2 83.3 %copy-start.48 = (f32[1,1024]{1,0:T(1,128)}, f32[1,1024]{1,0:T(1,128)S(1)}, u32[]{:S(2)}) copy-start(f32[1,1024]{1,0:T(1,128)S(1)} %get-tuple-element.28) | copy-start | bytes 12292
  202.9 34.8 %copy-start.36 = (f32[1024]{0:T(1024)}, f32[1024]{0:T(1024)S(1)}, u32[]{:S(2)}) copy-start(f32[1024]{0:T(1024)S(1)} %broadcast_multiply_fusion) | copy-start | bytes 12292
  205.4 32.3 %copy-start.38 = (f32[1024]{0:T(1024)}, f32[1024]{0:T(1024)S(1)}, u32[]{:S(2)}) copy-start(f32[1024]{0:T(1024)S(1)} %multiply_reduce_fusion.5) | copy-start | bytes 12292
  220.5 78.7 %copy-start.20 = (bf16[1024,1024]{1,0:T(8,128)(2,1)S(1)}, bf16[1024,1024]{1,0:T(8,128)(2,1)}, u32[]{:S(2)}) copy-start(bf16[1024,1024]{1,0:T(8,128)(2,1)} %fusion.10) | copy-start | bytes 6291460
  299.2 52.0 %copy-start.11 = (f32[1024,1024]{1,0:T(8,128)S(1)}, f32[1024,1024]{1,0:T(8,128)}, u32[]{:S(2)}) copy-start(f32[1024,1024]{1,0:T(8,128)} %copy-done.10) | copy-start | bytes 12582916
  299.2 52.0 %copy-start.37 = (f32[1024]{0:T(1024)S(1)}, f32[1024]{0:T(1024)}, u32[]{:S(2)}) copy-start(f32[1024]{0:T(1024)} %copy-done.36) | copy-start | bytes 12292
  299.2 52.0 %copy-start.42 = (f32[1024]{0:T(1024)S(1)}, f32[1024]{0:T(1024)}, u32[]{:S(2)}) copy-start(f32[1024]{0:T(1024)} %copy-done.41) | copy-start | bytes 12292
  299.3 52.0 %copy-start.44 = (f32[1,1024]{1,0:T(1,128)S(1)}, f32[1,1024]{1,0:T(1,128)}, u32[]{:S(2)}) copy-start(f32[1,1024]{1,0:T(1,128)} %copy-done.43) | copy-start | bytes 12292
  428.9 265.4 %reduce-scatter.21.cloned.1.call-start = ((), (), s32[]{:S(2)}) async-start(), calls=%async_computation.15 | async-start | bytes 540672
  430.7 405.1 %reduce-scatter.13.cloned.1.call-start = ((), (), s32[]{:S(2)}) async-start(), calls=%async_computation.11 | async-start | bytes 4325376 | tf_op jit(solution)/shard_map/reduce_scatter | solution.py:169
  437.3 557.5 %reduce-scatter.11.cloned.1.call-start = ((), (), s32[]{:S(2)}) async-start(), calls=%async_computation.10 | async-start | bytes 12976128 | tf_op jit(solution)/shard_map/reduce_scatter | solution.py:168
  449.5 733.9 %reduce-scatter.15.cloned.1.call-start = ((), (), s32[]{:S(2)}) async-start(), calls=%async_computation.12 | async-start | bytes 17301504 | tf_op jit(solution)/shard_map/reduce_scatter | solution.py:112
  467.1 903.6 %reduce-scatter.17.cloned.1.call-start = ((), (), s32[]{:S(2)}) async-start(), calls=%async_computation.13 | async-start | bytes 17301504 | tf_op jit(solution)/shard_map/reduce_scatter | solution.py:113
  494.2 41.0 %copy-start.35 = (f32[1,2,4,128]{3,1,2,0:T(2,128)S(1)}, f32[1,2,4,128]{3,1,2,0:T(2,128)}, u32[]{:S(2)}) copy-start(f32[1,2,4,128]{3,1,2,0:T(2,128)} %copy-done.34) | copy-start | bytes 12292
  (46 other events, 247.4 us)
Sparse Core Ops, SparseCore 0:
  11.1 72.1 all-gather.7
  86.2 55.0 all-gather.9
  144.3 76.1 all-gather.11
  223.4 75.8 all-gather.13
  429.0 132.5 reduce-scatter.18
  563.7 130.4 reduce-scatter.20
  697.1 138.6 reduce-scatter.12
  842.4 152.3 reduce-scatter.10
  997.7 185.6 reduce-scatter.14
  1186.3 184.3 reduce-scatter.16
where the time goes:
time: 1390 us; the launch traced here: 1380 us
  waiting for transfers between devices  890 us (64%)
  matrix products  197 us (14%)
  blocking collectives  158 us (11%)
  local copies, waits for them, and re-layouts  76.6 us (6%)
  other arithmetic  39.9 us (3%)
  between operations  15.3 us (1%)
    reduce_scatter x1, waiting for transfers between devices, body(): lax.psum_scatter(grad_fc_local, ('win', 'seq'), scatter_dimension=0, tile...  189 us
    reduce_scatter x1, waiting for transfers between devices, body(): lax.psum_scatter(grad_down_local, ('win', 'seq'), scatter_dimension=0, ti...  187 us
    reduce_scatter x1, waiting for transfers between devices, body(): lax.psum_scatter(grad_qkv_local, ('win', 'seq'), scatter_dimension=0, til...  159 us
    reduce_scatter x1, waiting for transfers between devices, body(): lax.psum_scatter(grad_out_local, ('win', 'seq'), scatter_dimension=0, til...  140 us
    unnamed x12, waiting for transfers between devices  139 us
    dot_general x4, matrix products, times_transposed(): lax.dot_general(first, second, (((1,), (1,)), ((), ())), preferred_elemen...  80.8 us
    all_gather x1, waiting for transfers between devices, body(): lax.all_gather(w_down, ('win', 'seq'), axis=0, tiled=True)  61.5 us
    dot_general x4, matrix products, outer_sum(): lax.dot_general(first, second, (((0,), (0,)), ((), ())), preferred_elemen...  47.1 us
  transfers between devices with their start and end apart: 10, of which 8 were waited for; matrix products, arithmetic and copies ran while one was open for 12% of the time, Pallas kernels for 0%

commit v1 on v0

--- a/solution.py
+++ b/solution.py
@@ -1,9 +1,247 @@
+import functools
 from functools import partial
 
 import jax
 import jax.numpy as jnp
 from jax import lax
+from jax.experimental import pallas as pl
+from jax.experimental.pallas import tpu as pltpu
 from jax.sharding import PartitionSpec as P
+
+MESH = pl.DeviceIdType.MESH
+ALL = slice(None)
+
+
+class Place:
+    def __init__(self):
+        win, seq = lax.axis_index("win"), lax.axis_index("seq")
+        self.y, self.x = win // 2, win % 2
+        self.z, self.c = seq // 2, seq % 2
+
+    def device(self, y=None, x=None, z=None, c=None):
+        y = self.y if y is None else y
+        x = self.x if x is None else x
+        z = self.z if z is None else z
+        c = self.c if c is None else c
+        return (y * 2 + x, z * 2 + c)
+
+    def partner(self, dim):
+        if dim == "x":
+            return self.device(x=1 - self.x)
+        if dim == "y":
+            return self.device(y=1 - self.y)
+        return self.device(c=1 - self.c)
+
+
+def greet(place):
+    barrier = pltpu.get_barrier_semaphore()
+    others = [place.partner(dim) for dim in "xyc"]
+    others += [place.device(z=(place.z + t) % 4) for t in (1, 2, 3)]
+    for device in others:
+        pl.semaphore_signal(barrier, inc=1, device_id=device, device_id_type=MESH)
+    pl.semaphore_wait(barrier, 6)
+
+
+def guarded(cond, thunk):
+    if cond is None:
+        thunk()
+    else:
+        pl.when(cond)(thunk)
+
+
+class Gather:
+    def __init__(self, place, view, order, send, recv, slack=0):
+        self.p, self.view, self.send, self.recv = place, view, send, recv
+        self.order, self.sent = order, []
+        self.ticks = self.plan(slack)
+
+    def region(self, got, **at):
+        p = self.p
+        pick = lambda d, own: at[d] if d in at else (ALL if d in got else own)
+        return self.view(pick("y", p.y), pick("x", p.x), pick("z", p.z), at.get("c", p.c))
+
+    def copy(self, region, device, number):
+        return pltpu.make_async_remote_copy(
+            region, region, self.send.at[number], self.recv.at[number],
+            device_id=device, device_id_type=MESH)
+
+    def push(self, cond, make, device, number):
+        def go():
+            self.copy(make(), device, number).start()
+        guarded(cond, go)
+
+        def end():
+            self.copy(make(), device, number).wait_send()
+        self.sent.append((cond, end))
+
+    def take(self, cond, make, number):
+        def go():
+            self.copy(make(), self.p.device(c=1 - self.p.c), number).wait_recv()
+        guarded(cond, go)
+
+    def both(self, cond, other):
+        return other if cond is None else jnp.logical_and(cond, other)
+
+    def line_push(self, got, cond):
+        for t in (1, 2, 3):
+            self.push(cond, lambda: self.region(got), self.p.device(z=(self.p.z + t) % 4), 1 + t)
+
+    def line_take(self, got, cond):
+        for t in (1, 2, 3):
+            self.take(cond, lambda t=t: self.region(got, z=(self.p.z + 4 - t) % 4), 1 + t)
+
+    def plan(self, slack):
+        out = []
+        p = self.p
+        orders = {0: (("xzy", None),), 1: (("yzx", None),),
+                  2: (("zxy", p.c == 0), ("zyx", p.c == 1))}[self.order]
+        lists = []
+        for order, cond in orders:
+            ticks = [[]]
+            got = ""
+            ex = 0
+            for dim in order:
+                if dim == "z":
+                    ticks[-1].append(functools.partial(self.line_push, got, cond))
+                    ticks.append([])
+                    ticks[-1].append(functools.partial(self.line_take, got, cond))
+                else:
+                    ticks[-1].append(functools.partial(
+                        self.push, cond, functools.partial(self.region, got), p.partner(dim), ex))
+                    if ex == 1:
+                        ticks.extend([] for _ in range(slack))
+                    ticks.append([])
+                    own = p.x if dim == "x" else p.y
+                    ticks[-1].append(functools.partial(
+                        self.take, cond, functools.partial(self.region, got, **{dim: 1 - own}), ex))
+                    ex += 1
+                got += dim
+            ticks[-1].append(functools.partial(self.push, cond, functools.partial(self.region, "xyz"),
+                                               p.partner("c"), 8))
+            ticks.append([])
+            ticks[-1].append(functools.partial(self.take, cond,
+                                               functools.partial(self.region, "xyz", c=1 - p.c), 8))
+            lists.append(ticks)
+        n = max(len(t) for t in lists)
+        for i in range(n):
+            thunks = [f for t in lists if i < len(t) for f in t[i]]
+            out.append(thunks)
+        return out
+
+    def tick(self, i):
+        for f in self.ticks[i]:
+            f()
+
+    def finish(self):
+        for cond, end in self.sent:
+            guarded(cond, end)
+
+
+def run_ticks(pieces, starts):
+    last = max(s + len(p.ticks) for p, s in zip(pieces, starts))
+    for now in range(last):
+        for p, s in zip(pieces, starts):
+            if 0 <= now - s < len(p.ticks):
+                p.tick(now - s)
+    for p in pieces:
+        p.finish()
+
+
+class Scatter:
+    def __init__(self, place, slot, bufs, order, send, recv, put):
+        self.p, self.slot, self.bufs, self.put = place, slot, bufs, put
+        self.send, self.recv, self.sent = send, recv, []
+        self.ticks = self.plan(order)
+
+    def region(self, left, **at):
+        p = self.p
+        pick = lambda d, own: at[d] if d in at else (ALL if d in left else own)
+        return self.slot.at[pick("y", p.y), pick("x", p.x), pick("z", p.z), at.get("c", p.c)]
+
+    def push(self, cond, make, buf, device, number):
+        def copy():
+            return pltpu.make_async_remote_copy(
+                make(), buf, self.send.at[number], self.recv.at[number],
+                device_id=device, device_id_type=MESH)
+        guarded(cond, lambda: copy().start())
+        self.sent.append((cond, lambda: copy().wait_send()))
+
+    def take(self, cond, makes, bufs, numbers, last):
+        def go():
+            for buf, number in zip(bufs, numbers):
+                pltpu.make_async_remote_copy(
+                    buf, buf, self.send.at[number], self.recv.at[number],
+                    device_id=self.p.partner("c"), device_id_type=MESH).wait_recv()
+            region = makes()
+            shape = region.shape
+            outer = [()]
+            while len(shape) - len(outer[0]) > 3:
+                outer = [o + (i,) for o in outer for i in range(shape[len(o)])]
+            for o in outer:
+                total = region[o + (Ellipsis,)].astype(jnp.float32)
+                for buf in bufs:
+                    total = total + buf[o + (Ellipsis,)].astype(jnp.float32)
+                if last:
+                    self.put(total)
+                else:
+                    region[o + (Ellipsis,)] = total.astype(region.dtype)
+        guarded(cond, go)
+
+    def plan(self, order):
+        p = self.p
+        core, first, second, line = self.bufs
+        variants = {0: (("yzx", None),), 1: (("xzy", None),),
+                    2: (("yxz", p.c == 0), ("xyz", p.c == 1))}[order]
+        ticks = [[] for _ in range(5)]
+        for dims, cond in variants:
+            left = "xyz"
+            ticks[0].append(functools.partial(
+                self.push, cond, lambda: self.region("xyz", c=1 - p.c), core, p.partner("c"), 0))
+            ticks[1].append(functools.partial(
+                self.take, cond, lambda: self.region("xyz"), [core], [0], False))
+            for i, dim in enumerate(dims):
+                rest = left.replace(dim, "")
+                last = i == 2
+                mine = functools.partial(self.region, rest)
+                if dim == "z":
+                    bufs = [line.at[t - 1] if rest else line.at[t - 1, 0] for t in (1, 2, 3)]
+                    for t in (1, 2, 3):
+                        to = (p.z + t) % 4
+                        ticks[i + 1].append(functools.partial(
+                            self.push, cond, functools.partial(self.region, rest, z=to),
+                            bufs[t - 1], p.device(z=to), 2 + t))
+                    ticks[i + 2].append(functools.partial(
+                        self.take, cond, mine, bufs, [3, 4, 5], last))
+                else:
+                    buf = first if i == 0 else (second if i == 1 else second.at[0])
+                    number = 1 if i == 0 else 2
+                    own = p.x if dim == "x" else p.y
+                    ticks[i + 1].append(functools.partial(
+                        self.push, cond, functools.partial(self.region, rest, **{dim: 1 - own}),
+                        buf, p.partner(dim), number))
+                    ticks[i + 2].append(functools.partial(
+                        self.take, cond, mine, [buf], [number], last))
+                left = rest
+        return ticks
+
+    def tick(self, i):
+        for f in self.ticks[i]:
+            f()
+
+    def finish(self):
+        for cond, end in self.sent:
+            guarded(cond, end)
+
+
+SCATTER_SEMS = 6
+GATHER_SEMS = 9
+
+
+def scatter_bufs(count, rows, cols, dtype=jnp.bfloat16):
+    return [pltpu.VMEM((count, 2, 2, 4, rows, cols), dtype), pltpu.VMEM((count, 2, 4, rows, cols), dtype),
+            pltpu.VMEM((count, 4, rows, cols), dtype), pltpu.VMEM((count, 3, 2, rows, cols), dtype),
+            pltpu.SemaphoreType.DMA((count, SCATTER_SEMS)), pltpu.SemaphoreType.DMA((count, SCATTER_SEMS))]
+
 
 HEADS = 16
 BLOCK = 128
@@ -38,7 +276,7 @@
     return jnp.where(causal, scores, -1e30)
 
 
-def body(
+def plain_body(
     tokens,
     condition,
     valid_mask,
@@ -183,9 +421,270 @@
     )
 
 
+GATHER_ORDER = (2, 0, 2, 2, 1, 2)
+
+
+def pack_small(gains, biases, fc_bias, rows, dtype):
+    devices = fc_bias.shape[0] // 128
+    eight = jnp.concatenate([gains, biases], axis=0)
+    eight = eight.reshape(8, devices, 32).transpose(1, 0, 2).reshape(devices, 2, 128)
+    packed = jnp.concatenate([eight, fc_bias.reshape(devices, 1, 128)], axis=1)
+    return jnp.pad(packed, ((0, 0), (0, rows - 3), (0, 0))).astype(dtype)
+
+
+def unpack_small(packed):
+    devices = packed.shape[0]
+    eight = packed[:, :2].reshape(devices, 8, 32).transpose(1, 0, 2).reshape(8, devices * 32)
+    return eight[:2], eight[2:], packed[:, 2].reshape(devices * 128)
+
+
+def gather_all(w_qkv, w_out, w_fc, w_down, norm_gains, biases, fc_bias):
+    small = pack_small(norm_gains, biases, fc_bias, 16, jnp.bfloat16)[0]
+    shards = (small, w_qkv, w_out, w_fc, w_down)
+    cuts = [(0, (0, 16), (0, 128))]
+    cuts += [(1, (0, 32), (i * 512, 512)) for i in range(6)]
+    cuts += [(2, (0, 32), (i * 512, 512)) for i in range(2)]
+    cuts += [(3, (0, 32), (i * 512, 512)) for i in range(8)]
+    cuts += [(4, (i * 16, 16), (0, 1024)) for i in range(8)]
+    count = len(cuts)
+
+    def kernel(*refs):
+        ins, fulls, (send, recv, local) = refs[:5], refs[5:10], refs[10:]
+        place = Place()
+        greet(place)
+        own = [
+            pltpu.make_async_copy(s, f.at[place.y, place.x, place.z, place.c], local.at[i])
+            for i, (s, f) in enumerate(zip(ins, fulls))
+        ]
+        for c in own:
+            c.start()
+        for c in own:
+            c.wait()
+
+        def make(k):
+            n, (r0, r), (c0, w) = cuts[k]
+            view = lambda y, x, z, c: fulls[n].at[y, x, z, c, pl.ds(r0, r), pl.ds(c0, w)]
+            return Gather(place, view, GATHER_ORDER[k % 6], send.at[k], recv.at[k], 1)
+
+        run_ticks([make(k) for k in range(count)], [(k + 2) // 3 for k in range(count)])
+
+    fulls = pl.pallas_call(
+        kernel,
+        out_shape=[jax.ShapeDtypeStruct((2, 2, 4, 2) + s.shape, s.dtype) for s in shards],
+        in_specs=[pl.BlockSpec(memory_space=pl.ANY)] * 5,
+        out_specs=[pl.BlockSpec(memory_space=pl.ANY)] * 5,
+        scratch_shapes=[
+            pltpu.SemaphoreType.DMA((count, GATHER_SEMS)),
+            pltpu.SemaphoreType.DMA((count, GATHER_SEMS)),
+            pltpu.SemaphoreType.DMA((5,)),
+        ],
+        compiler_params=pltpu.CompilerParams(collective_id=0, has_side_effects=True),
+    )(*shards)
+    mats = [f.reshape(-1, f.shape[-1]) for f in fulls[1:]]
+    return (*mats, *unpack_small(fulls[0].reshape(32, 16, 128)))
+
+
+def scatter_all(g_qkv, g_out, g_fc, g_down, gains, biases, fc_bias):
+    small = pack_small(gains, biases, fc_bias, 8, jnp.float32)
+    full = [g.astype(jnp.bfloat16) for g in (g_qkv, g_out, g_fc, g_down)]
+    shapes = [(g.shape[0] // 32, g.shape[1]) for g in full]
+    cuts = [
+        (n, (r0, 32), (c0, 512))
+        for n, (rows, cols) in enumerate(shapes)
+        for r0 in range(0, rows, 32)
+        for c0 in range(0, cols, 512)
+    ]
+    count, depth = len(cuts), 18
+
+    def kernel(*refs):
+        ins, outs, (slots, own, load_sem), rest = refs[:5], refs[5:10], refs[10:13], refs[13:]
+        big, little = rest[:6], rest[6:]
+        place = Place()
+        greet(place)
+
+        def make(k):
+            n, (r0, r), (c0, w) = cuts[k]
+
+            def put(value):
+                outs[n + 1][pl.ds(r0, r), pl.ds(c0, w)] = value
+
+            return Scatter(place, slots.at[k % depth], [b.at[k] for b in big[:4]],
+                           GATHER_ORDER[k % 6], big[4].at[k], big[5].at[k], put)
+
+        def put_small(value):
+            outs[0][...] = value
+
+        def load(k):
+            n, (r0, r), (c0, w) = cuts[k]
+            return pltpu.make_async_copy(
+                ins[n + 1].at[:, :, :, :, pl.ds(r0, r), pl.ds(c0, w)],
+                slots.at[k % depth], load_sem.at[k % depth])
+
+        small_load = pltpu.make_async_copy(ins[0], own, load_sem.at[depth])
+        small_load.start()
+        pieces = [Scatter(place, own, [b.at[0] for b in little[:4]], 2,
+                          little[4].at[0], little[5].at[0], put_small)]
+        pieces += [make(k) for k in range(count)]
+        loads = [small_load] + [load(k) for k in range(count)]
+        groups = [[0, 1, 2, 3]] + [list(range(i, min(i + 3, count + 1))) for i in range(4, count + 1, 3)]
+        for k in groups[0][1:]:
+            loads[k].start()
+        for now in range(len(groups) + 4):
+            if now + 1 < len(groups):
+                for k in groups[now + 1]:
+                    loads[k].start()
+            for age in range(4, -1, -1):
+                if 0 <= now - age < len(groups):
+                    for k in groups[now - age]:
+                        if age == 0:
+                            loads[k].wait()
+                        pieces[k].tick(age)
+                        if age == 4:
+                            pieces[k].finish()
+
+    out = pl.pallas_call(
+        kernel,
+        out_shape=[jax.ShapeDtypeStruct(s, jnp.float32) for s in [(8, 128)] + shapes],
+        in_specs=[pl.BlockSpec(memory_space=pl.ANY)] * 5,
+        out_specs=[pl.BlockSpec(memory_space=pltpu.VMEM)] * 5,
+        scratch_shapes=[pltpu.VMEM((depth, 2, 2, 4, 2, 32, 512), jnp.bfloat16),
+                        pltpu.VMEM((2, 2, 4, 2, 8, 128), jnp.float32),
+                        pltpu.SemaphoreType.DMA((depth + 1,))]
+        + scatter_bufs(count, 32, 512) + scatter_bufs(1, 8, 128, jnp.float32),
+        compiler_params=pltpu.CompilerParams(
+            collective_id=1, has_side_effects=True, vmem_limit_bytes=60 << 20),
+    )(small.reshape(2, 2, 4, 2, 8, 128),
+      *[g.reshape((2, 2, 4, 2) + s) for g, s in zip(full, shapes)])
+    return (*out[1:], *unpack_small(out[0][None]))
+
+
+def body(
+    tokens,
+    condition,
+    valid_mask,
+    w_qkv,
+    w_out,
+    w_fc,
+    w_down,
+    norm_gains,
+    biases,
+    fc_bias,
+    cotangent,
+):
+    window_count, span_rows, model_width = tokens.shape
+    row_total = window_count * span_rows
+    head_size = model_width // HEADS
+    head_shape = (row_total // BLOCK, BLOCK, HEADS, head_size)
+    keep_rows = valid_mask.reshape(row_total, 1).astype(jnp.float32)
+    hidden = tokens.reshape(row_total, model_width).astype(jnp.float32) + condition.reshape(
+        row_total, model_width
+    ).astype(jnp.float32)
+    full_qkv, full_out, full_fc, full_down, full_gains, full_biases, full_fc_bias = gather_all(
+        w_qkv, w_out, w_fc, w_down, norm_gains, biases, fc_bias
+    )
+    gain_f = full_gains.astype(jnp.float32)
+    bias_f = full_biases.astype(jnp.float32)
+    normed_f, norm_back_one = jax.vjp(layer_norm, hidden, gain_f[0], bias_f[0])
+    normed = normed_f.astype(jnp.bfloat16)
+    projected = jnp.dot(normed, full_qkv, preferred_element_type=jnp.float32)
+    queries = (projected[:, :model_width] + bias_f[1]).astype(jnp.bfloat16).reshape(head_shape)
+    key_rows = projected[:, model_width : 2 * model_width].astype(jnp.bfloat16).reshape(head_shape)
+    values = (projected[:, 2 * model_width :] + bias_f[2]).astype(jnp.bfloat16).reshape(head_shape)
+    scores = masked_scores(queries, key_rows)
+    row_max = jnp.max(scores, axis=-1, keepdims=True)
+    log_total = row_max + jnp.log(jnp.sum(jnp.exp(scores - row_max), axis=-1, keepdims=True))
+    probs = jnp.exp(scores - log_total).astype(jnp.bfloat16)
+    mixed = jnp.einsum("bhqk,bkhd->bqhd", probs, values, preferred_element_type=jnp.float32)
+    mixed = mixed.reshape(row_total, model_width).astype(jnp.bfloat16)
+    after_attn = hidden + jnp.dot(mixed, full_out, preferred_element_type=jnp.float32) + bias_f[3]
+    normed_two_f, norm_back_two = jax.vjp(layer_norm, after_attn, gain_f[1], bias_f[4])
+    normed_two = normed_two_f.astype(jnp.bfloat16)
+    pre_gelu = jnp.dot(
+        normed_two, full_fc, preferred_element_type=jnp.float32
+    ) + full_fc_bias.astype(jnp.float32)
+    gelu_f, gelu_back = jax.vjp(partial(jax.nn.gelu, approximate=False), pre_gelu)
+    gelu_out = gelu_f.astype(jnp.bfloat16)
+    final_rows = (
+        after_attn + jnp.dot(gelu_out, full_down, preferred_element_type=jnp.float32) + bias_f[5]
+    )
+    output = (final_rows * keep_rows).astype(jnp.bfloat16).reshape(tokens.shape)
+    back_fc, back_down, back_qkv, back_out = full_fc, full_down, full_qkv, full_out
+    grad_final = cotangent.reshape(row_total, model_width).astype(jnp.float32) * keep_rows
+    grad_mlp = grad_final.astype(jnp.bfloat16)
+    grad_down_local = outer_sum(gelu_out, grad_mlp)
+    grad_down_bias = jnp.sum(grad_mlp.astype(jnp.float32), axis=0)
+    grad_gelu = times_transposed(grad_mlp, back_down)
+    grad_pre = gelu_back(grad_gelu)[0].astype(jnp.bfloat16)
+    grad_fc_local = outer_sum(normed_two, grad_pre)
+    grad_fc_bias_local = jnp.sum(grad_pre.astype(jnp.float32), axis=0)
+    grad_normed_two = times_transposed(grad_pre, back_fc)
+    grad_after_norm, grad_gain_two, grad_shift_two = norm_back_two(grad_normed_two)
+    grad_after = grad_final + grad_after_norm
+    grad_attn = grad_after.astype(jnp.bfloat16)
+    grad_out_local = outer_sum(mixed, grad_attn)
+    grad_out_bias = jnp.sum(grad_attn.astype(jnp.float32), axis=0)
+    grad_mixed = times_transposed(grad_attn, back_out).astype(jnp.bfloat16).reshape(head_shape)
+    probs_full = jnp.exp(masked_scores(queries, key_rows) - log_total)
+    grad_probs = jnp.einsum(
+        "bqhd,bkhd->bhqk", grad_mixed, values, preferred_element_type=jnp.float32
+    )
+    grad_values = jnp.einsum(
+        "bhqk,bqhd->bkhd", probs, grad_mixed, preferred_element_type=jnp.float32
+    )
+    grad_values = grad_values.reshape(row_total, model_width).astype(jnp.bfloat16)
+    grad_scores = probs_full * (
+        grad_probs - jnp.sum(probs_full * grad_probs, axis=-1, keepdims=True)
+    )
+    grad_scores = grad_scores.astype(jnp.bfloat16)
+    grad_queries = (
+        jnp.einsum("bhqk,bkhd->bqhd", grad_scores, key_rows, preferred_element_type=jnp.float32)
+        * 0.125
+    )
+    grad_keys = (
+        jnp.einsum("bhqk,bqhd->bkhd", grad_scores, queries, preferred_element_type=jnp.float32)
+        * 0.125
+    )
+    grad_queries = grad_queries.reshape(row_total, model_width).astype(jnp.bfloat16)
+    grad_keys = grad_keys.reshape(row_total, model_width).astype(jnp.bfloat16)
+    grad_query_bias = jnp.sum(grad_queries.astype(jnp.float32), axis=0)
+    grad_value_bias = jnp.sum(grad_values.astype(jnp.float32), axis=0)
+    grad_projected = jnp.concatenate([grad_queries, grad_keys, grad_values], axis=1)
+    grad_qkv_local = outer_sum(normed, grad_projected)
+    grad_normed = times_transposed(grad_projected, back_qkv)
+    grad_hidden_norm, grad_gain_one, grad_shift_one = norm_back_one(grad_normed)
+    grad_input = (grad_after + grad_hidden_norm).astype(jnp.bfloat16).reshape(tokens.shape)
+    gains_local = jnp.stack([grad_gain_one, grad_gain_two])
+    biases_local = jnp.stack(
+        [
+            grad_shift_one,
+            grad_query_bias,
+            grad_value_bias,
+            grad_out_bias,
+            grad_shift_two,
+            grad_down_bias,
+        ]
+    )
+    grad_w_qkv, grad_w_out, grad_w_fc, grad_w_down, grad_gains, grad_biases, grad_fc_bias = scatter_all(
+        grad_qkv_local, grad_out_local, grad_fc_local, grad_down_local,
+        gains_local, biases_local, grad_fc_bias_local,
+    )
+    return (
+        output,
+        grad_input,
+        grad_w_qkv,
+        grad_w_out,
+        grad_w_fc,
+        grad_w_down,
+        grad_gains,
+        grad_biases,
+        grad_fc_bias,
+    )
+
+
 def solution(mesh):
+    fast = mesh.shape["win"] == 4 and mesh.shape["seq"] == 8
     return jax.shard_map(
-        body,
+        body if fast else plain_body,
         mesh=mesh,
         in_specs=(
             P("win", "seq", None),

time: 1390 us -> 580 us (0.42)
  waiting for transfers between devices: 890 us -> 0 us
  Pallas kernels: 0 us -> 269 us
  blocking collectives: 158 us -> 0 us
  matrix products: 197 us -> 181 us
    reduce_scatter x4 -> x0, waiting for transfers between devices: 675 us -> none  [the longest x1 189 us: body(): lax.psum_scatter(grad_fc_local, ('win', 'seq'), scatter_dimension=0, tile...]
    pallas_call x0 -> x2, Pallas kernels: none -> 269 us  [the longest x1 146 us: gather_all(): pl.pallas_call(kernel, out_shape=[jax.ShapeDtypeStruct((2, 2, 4, 2) + s.s...]
    unnamed x12 -> x0, waiting for transfers between devices: 139 us -> none
    all_gather x3 -> x0, blocking collectives: 118 us -> none  [the longest x1 43.1 us: body(): lax.all_gather(norm_gains, ('win', 'seq'), axis=1, tiled=True)]
    all_gather x4 -> x0, waiting for transfers between devices: 76.6 us -> none  [the longest x1 61.5 us: body(): lax.all_gather(w_down, ('win', 'seq'), axis=0, tiled=True)]
    unnamed x1 -> x0, blocking collectives: 39.7 us -> none
  transfers between devices with their start and end apart: 10 -> 0, of which waited for: 8 -> 0; matrix products, arithmetic and copies ran while one was open for 12% -> 0% of each run, Pallas kernels for 0% -> 0%
where the time goes in v1:
time: 580 us; the launch traced here: 574 us
  Pallas kernels  269 us (46%)
  matrix products  181 us (31%)
  local copies, waits for them, and re-layouts  75.3 us (13%)
  other arithmetic  47.1 us (8%)
    pallas_call x1, Pallas kernels, gather_all(): pl.pallas_call(kernel, out_shape=[jax.ShapeDtypeStruct((2, 2, 4, 2) + s.s...  146 us
    pallas_call x1, Pallas kernels, scatter_all(): pl.pallas_call(kernel, out_shape=[jax.ShapeDtypeStruct(s, jnp.float32) fo...  122 us
    dot_general x4, matrix products, times_transposed(): lax.dot_general(first, second, (((1,), (1,)), ((), ())), preferred_elemen...  82.5 us
    dot_general x4, matrix products, outer_sum(): lax.dot_general(first, second, (((0,), (0,)), ((), ())), preferred_elemen...  39.1 us
    unnamed x121, local copies, waits for them, and re-layouts  16.1 us
    dot_general x1, matrix products, body(): jnp.dot(gelu_out, full_down, preferred_element_type=jnp.float32)  14.8 us
    dot_general x1, matrix products, body(): jnp.dot(normed_two, full_fc, preferred_element_type=jnp.float32)  12.3 us
    reshape x2, local copies, waits for them, and re-layouts, body(): (projected[:, :model_width] + bias_f[1]).astype(jnp.bfloat16)  12.2 us

profile of v1, /device:TPU:0, one launch (start us, length us, event | category | flops | bytes accessed | tf_op | source)
XLA Modules:
  0.0 573.9 jit_solution(17408716693026799380)
XLA Ops:
  11.3 146.3 %shard_map.178 = (bf16[2,2,4,2,16,128]{5,4,3,2,1,0:T(8,128)(2,1)}, bf16[2,2,4,2,32,3072]{5,4,3,2,1,0:T(8,128)(2,1)}, bf16[2,2,4,2,32,1024]{5,4,3,2,1,0:T(8,128)(...) custom-call(bf16[16,128]{1,0:T(8,128)(2,1)} %fusion.29.refs_0_, bf16[32,3072]{1,0:T(8,128)(2,1)} %refs_1_.1, ...), custom_call_target="tpu_custom_call" | custom-call | tf_op jit(solution)/shard_map/pallas_call | solution.py:471
  161.1 4.1 add_convert_fusion.4
  165.3 6.7 %fusion.43 = f32[1024,3072]{1,0:T(8,128)S(1)} fusion(bf16[1024,1024]{1,0:T(8,128)(2,1)S(1)} %bitcast.138, bf16[1024,3072]{1,0:T(8,128)(2,1)S(1)} %bitcast.167), kind=kOutput, calls=%fused_computation.116 | convolution fusion | flops 6442450944 | bytes 20971520 | tf_op jit(solution)/shard_map/dot_general | solution.py:589
  175.6 6.4 %reshape.297 = bf16[8,128,16,64]{3,2,1,0:T(8,128)(2,1)} reshape(bf16[1024,1024]{1,0:T(8,128)(2,1)} %get-tuple-element.54) | data formatting | bytes 4194304 | tf_op jit(solution)/shard_map/reshape | solution.py:590
  182.0 5.8 %copy.35 = bf16[8,128,16,64]{1,3,2,0:T(8,128)(2,1)} copy(bf16[8,128,16,64]{3,2,1,0:T(8,128)(2,1)} %reshape.297) | data formatting | bytes 4194304 | tf_op jit(solution)/shard_map/reshape | solution.py:590
  191.8 5.9 %copy.36 = bf16[8,128,16,64]{1,3,2,0:T(8,128)(2,1)} copy(bf16[8,128,16,64]{3,2,1,0:T(8,128)(2,1)} %reshape.298) | data formatting | bytes 4194304 | tf_op jit(solution)/shard_map/reshape | solution.py:591
  197.8 4.0 reshape.296
  201.8 5.1 copy.37
  206.9 4.8 fusion.41
  222.9 12.3 %fusion.35 = f32[1024,4096]{1,0:T(8,128)S(1)} fusion(bf16[1024,4096]{1,0:T(8,128)(2,1)} %bitcast.164, f32[1024,1024]{1,0:T(8,128)S(1)} %get-tuple-element.70, f32[1024]{0:T(1024)S(1)} %add.148, f32[1024]{0:T(1024)S(1)} %mul.199, f32[1024]{0:T(1024)S(1)} %fusion.30, f32[1024]{0:T(1024)S(1)} %broadcast_multiply_fusion), kind=kOutput, calls=%fused_computation.110 | convolution fusion | flops 8595177472 | bytes 29376512 | tf_op jit(solution)/shard_map/dot_general | solution.py:602
  235.3 51.1 %convert_reduce_fusion = (f32[4096]{0:T(1024)}, bf16[1024,4096]{1,0:T(8,128)(2,1)}, f32[1024,4096]{1,0:T(8,128)}) fusion(f32[1024,4096]{1,0:T(8,128)S(1)} %fusion.35, f32[4096]{0:T(1024)S(1)} %bitcast.147, bf16[1024,1024]{1,0:T(8,128)(2,1)S(1)} %bitcast.139, bf16[4096,1024]{1,0:T(8,128)(2,1)} %bitcast.162), kind=kOutput, calls=%fused_computation.2 | convolution fusion | flops 8904503296 | bytes 52461568 | tf_op jit(solution)/shard_map/dot_general | solution.py:264
  286.4 16.8 %multiply_reduce_fusion.1 = (f32[1024]{0:T(1024)S(1)}, f32[1024]{0:T(1024)S(1)}, f32[1024]{0:T(1024)S(1)}, f32[1024,1024]{1,0:T(8,128)}) fusion(f32[1024,1024]{1,0:T(8,128)} %copy-done.10, f32[1024]{0:T(1024)} %copy-done.42, f32[1024]{0:T(1024)} %copy-done.31, f32[1024]{0:T(1024)S(1)} %copy-done.41, bf16[1024,4096]{1,0:T(8,128)(2,1)} %get-tuple-element.48, ...), kind=kOutput, calls=%fused_computation.44 | convolution fusion | flops 8598320128 | bytes 25190400 | tf_op jit(solution)/shard_map/dot_general | solution.py:264
  303.2 11.1 %multiply_convert_fusion = bf16[1024,4096]{1,0:T(8,128)(2,1)} fusion(f32[1024,4096]{1,0:T(8,128)} %get-tuple-element.49, f32[1024,4096]{1,0:T(8,128)S(1)} %fusion.35, f32[4096]{0:T(1024)S(1)} %bitcast.148), kind=kLoop, calls=%fused_computation.4 | loop fusion | flops 16777216 | bytes 41959424 | tf_op jit(solution)/shard_map/convert_element_type | solution.py:606
  314.3 14.8 %multiply_convert_fusion.5 = bf16[1024,1024]{1,0:T(8,128)(2,1)} fusion(f32[1024,1024]{1,0:T(8,128)S(1)} %copy-done.11, f32[1024]{0:T(1024)S(1)} %bitcast.151, f32[1024]{0:T(1024)S(1)} %copy-done.50, bf16[1024,4096]{1,0:T(8,128)(2,1)} %multiply_convert_fusion, bf16[4096,1024]{1,0:T(8,128)(2,1)} %bitcast.163), kind=kOutput, calls=%fused_computation.53 | convolution fusion | flops 8594128896 | bytes 23076864 | tf_op jit(solution)/shard_map/dot_general | solution.py:608
  332.2 15.3 %convolution_convert_fusion.1 = bf16[1024,4096]{1,0:T(8,128)(2,1)} fusion(bf16[1024,4096]{1,0:T(8,128)(2,1)} %get-tuple-element.48, f32[1024,1024]{1,0:T(8,128)S(1)} %copy-done.12, f32[1024]{0:T(1024)S(1)} %copy-done.49, f32[1024]{0:T(1024)S(1)} %copy-done.41, f32[1024]{0:T(1024)S(1)} %copy-done.43, f32[1024]{0:T(1024)S(1)} %copy-done.32), kind=kOutput, calls=%fused_computation.25 | convolution fusion | flops 8599371776 | bytes 20987904 | tf_op jit(solution)/shard_map/dot_general | solution.py:258
  357.0 4.0 reshape.299
  361.1 5.2 copy.41
  367.6 6.4 %convert_reduce_fusion.3 = (f32[16,64]{1,0:T(8,128)S(1)}, bf16[8,16,64,128]{3,2,1,0:T(8,128)(2,1)S(1)}) fusion(bf16[8,128,16,64]{1,3,2,0:T(8,128)(2,1)S(1)} %copy.41, f32[8,16,128,128]{2,3,1,0:T(8,128)} %copy-done, f32[8,16,128]{2,1,0:T(8,128)S(1)} %copy-done.25), kind=kOutput, calls=%fused_computation.42 | convolution fusion | flops 275774464 | bytes 12652544 | tf_op jit(solution)/shard_map/bhqk,bqhd->bkhd/dot_general | solution.py:631
  377.3 6.3 %multiply_reduce_fusion = (f32[8,16,128]{2,1,0:T(8,128)S(1)}, f32[8,16,128,128]{2,3,1,0:T(8,128)S(1)}) fusion(f32[8,16,128,128]{2,3,1,0:T(8,128)} %copy-done, f32[8,16,128]{2,1,0:T(8,128)S(1)} %copy-done.25, bf16[8,128,16,64]{1,3,2,0:T(8,128)(2,1)} %copy-done.6, bf16[8,128,16,64]{1,3,2,0:T(8,128)(2,1)S(1)} %copy-done.5), kind=kOutput, calls=%fused_computation.19 | convolution fusion | flops 274710528 | bytes 21102592 | tf_op jit(solution)/shard_map/bqhd,bkhd->bhqk/dot_general | solution.py:628
  383.7 5.3 multiply_convert_fusion.1
  402.4 12.3 %multiply_reduce_fusion.2 = (f32[1024]{0:T(1024)S(1)}, f32[1024]{0:T(1024)S(1)}, f32[1024]{0:T(1024)S(1)}, f32[1024,1024]{1,0:T(8,128)S(1)}) fusion(f32[4,256,1024]{2,1,0:T(8,128)S(1)} %copy-done.14, f32[1024]{0:T(1024)S(1)} %bitcast.155, f32[1024]{0:T(1024)S(1)} %copy-done.46, f32[1024]{0:T(1024)S(1)} %copy-done.36, ...), kind=kOutput, calls=%fused_computation.45 | convolution fusion | flops 6450836480 | bytes 20996096 | tf_op jit(solution)/shard_map/dot_general | solution.py:264
  417.5 8.7 %convolution_convert_fusion.2 = bf16[1024,3072]{1,0:T(8,128)(2,1)} fusion(bf16[1024,1024]{1,0:T(8,128)(2,1)S(1)} %get-tuple-element.56, bf16[1024,3072]{0,1:T(8,128)(2,1)S(1)} %copy-done.27), kind=kOutput, calls=%fused_computation.29 | convolution fusion | flops 6445596672 | bytes 14680064 | tf_op jit(solution)/shard_map/dot_general | solution.py:258
  428.4 11.5 %convolution_convert_fusion = bf16[4096,1024]{1,0:T(8,128)(2,1)} fusion(bf16[1024,4096]{1,0:T(8,128)(2,1)S(1)} %bitcast.129, bf16[1024,1024]{1,0:T(8,128)(2,1)S(1)} %get-tuple-element.59), kind=kOutput, calls=%fused_computation.24 | convolution fusion | flops 8594128896 | bytes 18874368 | tf_op jit(solution)/shard_map/dot_general | solution.py:258
  441.1 122.2 %shard_map.179 = (f32[8,128]{1,0:T(8,128)}, f32[32,3072]{1,0:T(8,128)}, f32[32,1024]{1,0:T(8,128)}, f32[32,4096]{1,0:T(8,128)}, f32[128,1024]{1,0:T(8,128)}) custom-call(f32[2,2,4,2,8,128]{5,4,3,2,1,0:T(8,128)} %bitcast.143, bf16[2,2,4,2,32,3072]{5,4,3,2,1,0:T(8,128)(2,1)} %bitcast.136, bf16[2,2,4,2,32,1024]{5,4,3,2,1,0:T(8,128)(2,1)} %bitcast.137, ...), custom_call_target="tpu_custom_call" | custom-call | tf_op jit(solution)/shard_map/pallas_call | solution.py:545
  (189 shorter events, 79.8 us)
Async XLA Ops:
  7.5 151.8 %copy-start.29 = (f32[1,2,4,128]{3,1,2,0:T(2,128)}, f32[1,2,4,128]{3,1,2,0:T(2,128)S(1)}, u32[]{:S(2)}) copy-start(f32[1,2,4,128]{3,1,2,0:T(2,128)S(1)} %copy.69) | copy-start | bytes 12292
  159.9 63.0 %copy-start.48 = (f32[1024]{0:T(1024)}, f32[1024]{0:T(1024)S(1)}, u32[]{:S(2)}) copy-start(f32[1024]{0:T(1024)S(1)} %add.148) | copy-start | bytes 12292
  160.0 62.9 %copy-start.40 = (f32[1024]{0:T(1024)}, f32[1024]{0:T(1024)S(1)}, u32[]{:S(2)}) copy-start(f32[1024]{0:T(1024)S(1)} %mul.199) | copy-start | bytes 12292
  221.3 13.9 %copy-start.10 = (f32[1024,1024]{1,0:T(8,128)}, f32[1024,1024]{1,0:T(8,128)S(1)}, u32[]{:S(2)}) copy-start(f32[1024,1024]{1,0:T(8,128)S(1)} %get-tuple-element.70) | copy-start | bytes 12582916
  221.3 13.9 %copy-start.31 = (f32[1024]{0:T(1024)}, f32[1024]{0:T(1024)S(1)}, u32[]{:S(2)}) copy-start(f32[1024]{0:T(1024)S(1)} %broadcast_multiply_fusion) | copy-start | bytes 12292
  222.9 12.3 %copy-start.42 = (f32[1024]{0:T(1024)}, f32[1024]{0:T(1024)S(1)}, u32[]{:S(2)}) copy-start(f32[1024]{0:T(1024)S(1)} %fusion.30) | copy-start | bytes 12292
  222.9 12.3 %copy-start.21 = (bf16[4,256,1024]{2,1,0:T(8,128)(2,1)S(1)}, bf16[4,256,1024]{2,1,0:T(8,128)(2,1)}, u32[]{:S(2)}) copy-start(bf16[4,256,1024]{2,1,0:T(8,128)(2,1)} %get-tuple-element.44) | copy-start | bytes 6291460
  235.3 51.1 %copy-start.41 = (f32[1024]{0:T(1024)S(1)}, f32[1024]{0:T(1024)}, u32[]{:S(2)}) copy-start(f32[1024]{0:T(1024)} %copy-done.40) | copy-start | bytes 12292
  286.4 16.8 %copy-start.34 = (f32[1024]{0:T(1024)S(1)}, f32[1024]{0:T(1024)}, u32[]{:S(2)}) copy-start(f32[1024]{0:T(1024)} %copy-done.33) | copy-start | bytes 12292
  303.1 11.1 %copy-start.11 = (f32[1024,1024]{1,0:T(8,128)S(1)}, f32[1024,1024]{1,0:T(8,128)}, u32[]{:S(2)}) copy-start(f32[1024,1024]{1,0:T(8,128)} %copy-done.10) | copy-start | bytes 12582916
  303.1 11.1 %copy-start.39 = (f32[1,2,4,128]{3,1,2,0:T(2,128)S(1)}, f32[1,2,4,128]{3,1,2,0:T(2,128)}, u32[]{:S(2)}) copy-start(f32[1,2,4,128]{3,1,2,0:T(2,128)} %copy.65) | copy-start | bytes 12292
  303.2 11.1 %copy-start.50 = (f32[1024]{0:T(1024)S(1)}, f32[1024]{0:T(1024)}, u32[]{:S(2)}) copy-start(f32[1024]{0:T(1024)} %add.154) | copy-start | bytes 12292
  314.2 14.8 %copy-start.20 = (f32[1024,1024]{1,0:T(8,128)S(1)}, f32[1024,1024]{1,0:T(8,128)}, u32[]{:S(2)}) copy-start(f32[1024,1024]{1,0:T(8,128)} %get-tuple-element.71) | copy-start | bytes 12582916
  314.3 14.8 %copy-start.32 = (f32[1024]{0:T(1024)S(1)}, f32[1024]{0:T(1024)}, u32[]{:S(2)}) copy-start(f32[1024]{0:T(1024)} %copy-done.31) | copy-start | bytes 12292
  314.3 14.8 %copy-start.43 = (f32[1024]{0:T(1024)S(1)}, f32[1024]{0:T(1024)}, u32[]{:S(2)}) copy-start(f32[1024]{0:T(1024)} %copy-done.42) | copy-start | bytes 12292
  332.2 15.5 %copy-start.8 = (bf16[4,256,1024]{2,1,0:T(8,128)(2,1)S(1)}, bf16[4,256,1024]{2,1,0:T(8,128)(2,1)}, u32[]{:S(2)}) copy-start(bf16[4,256,1024]{2,1,0:T(8,128)(2,1)} %param.21) | copy-start | bytes 6291460
  402.3 12.3 %copy-start.26 = (bf16[1024,3072]{0,1:T(8,128)(2,1)}, bf16[1024,3072]{0,1:T(8,128)(2,1)S(1)}, u32[]{:S(2)}) copy-start(bf16[1024,3072]{0,1:T(8,128)(2,1)S(1)} %bitcast_dynamic-update-slice_fusion) | copy-start | bytes 18874372
  402.3 12.3 %copy-start.30 = (f32[1,2,4,128]{3,1,2,0:T(2,128)S(1)}, f32[1,2,4,128]{3,1,2,0:T(2,128)}, u32[]{:S(2)}) copy-start(f32[1,2,4,128]{3,1,2,0:T(2,128)} %copy-done.29) | copy-start | bytes 12292
  402.4 12.4 %copy-start.38 = (f32[1024]{0:T(1024)S(1)}, f32[1024]{0:T(1024)}, u32[]{:S(2)}) copy-start(f32[1024]{0:T(1024)} %copy-done.37) | copy-start | bytes 12292
  414.7 13.7 %slice-start = ((s8[8388608]{0:T(1024)(128)(4,1)}), s8[4194304]{0:T(1024)(128)(4,1)S(1)}, s32[]{:S(2)}) async-start(s8[8388608]{0:T(1024)(128)(4,1)} %bitcast.128), calls=%async_computation | async-start | bytes 8388608
  417.5 8.7 %copy-start.9 = (bf16[4,256,1024]{2,1,0:T(8,128)(2,1)S(1)}, bf16[4,256,1024]{2,1,0:T(8,128)(2,1)}, u32[]{:S(2)}) copy-start(bf16[4,256,1024]{2,1,0:T(8,128)(2,1)} %param.21) | copy-start | bytes 6291460
  417.5 10.9 %slice-start.1 = ((s8[8388608]{0:T(1024)(128)(4,1)}), s8[4194304]{0:T(1024)(128)(4,1)S(1)}, s32[]{:S(2)}) async-start(s8[8388608]{0:T(1024)(128)(4,1)} %bitcast.128), calls=%async_computation.1 | async-start | bytes 8388608
  428.4 11.7 %copy-start.28 = (f32[1,32,32]{2,0,1:T(1,128)S(1)}, f32[1,32,32]{2,0,1:T(1,128)}, u32[]{:S(2)}) copy-start(f32[1,32,32]{2,0,1:T(1,128)} %concatenate.42) | copy-start | bytes 12292
  428.4 12.0 %copy-start.44 = (f32[4096]{0:T(1024)S(1)}, f32[4096]{0:T(1024)}, u32[]{:S(2)}) copy-start(f32[4096]{0:T(1024)} %get-tuple-element.47) | copy-start | bytes 49156
  (32 other events, 120.6 us)

commit v2 on v1

--- a/solution.py
+++ b/solution.py
@@ -178,9 +178,11 @@
             while len(shape) - len(outer[0]) > 3:
                 outer = [o + (i,) for o in outer for i in range(shape[len(o)])]
             for o in outer:
-                total = region[o + (Ellipsis,)].astype(jnp.float32)
+                many = last or len(bufs) > 1
+                total = region[o + (Ellipsis,)]
+                total = total.astype(jnp.float32) if many else total
                 for buf in bufs:
-                    total = total + buf[o + (Ellipsis,)].astype(jnp.float32)
+                    total = total + buf[o + (Ellipsis,)].astype(total.dtype)
                 if last:
                     self.put(total)
                 else:
@@ -243,6 +245,198 @@
             pltpu.SemaphoreType.DMA((count, SCATTER_SEMS)), pltpu.SemaphoreType.DMA((count, SCATTER_SEMS))]
 
 
+D, FF, CH = 1024, 4096, 512
+DELAY = (0, 1, 4, 6, 8)
+TILE = 256
+
+
+def dot_nn(a, b):
+    return lax.dot_general(a, b, (((1,), (0,)), ((), ())), preferred_element_type=jnp.float32)
+
+
+def dot_nt(a, b):
+    return lax.dot_general(a, b, (((1,), (1,)), ((), ())), preferred_element_type=jnp.float32)
+
+
+def dot_tn(a, b):
+    return lax.dot_general(a, b, (((0,), (0,)), ((), ())), preferred_element_type=jnp.float32)
+
+
+def norm_stats(rows_in):
+    mean = jnp.mean(rows_in, axis=-1, keepdims=True)
+    centered = rows_in - mean
+    var = jnp.mean(centered * centered, axis=-1, keepdims=True)
+    rstd = lax.rsqrt(var + 1e-05)
+    return centered * rstd, rstd
+
+
+def gelu_both(v):
+    phi = 0.5 + 0.5 * lax.erf(v * 0.7071067811865476)
+    slope = phi + v * (jnp.exp(-0.5 * v * v) * 0.3989422804014327)
+    return (v * phi).astype(jnp.bfloat16), slope
+
+
+def mlp_kernel(comm, after_hbm, cot_hbm, mask_ref, vec_ref, fcb_ref, wfc_hbm, wdn_hbm,
+               out_ref, gafter_hbm, gdown_hbm, gfc_ref, small_ref, gfcb_ref,
+               after, gm, n2, n2t, gelu, gp, fin, gn2, wfc, wdn, stage, slots, lsem, wsem, ssem, *rest):
+    place = Place()
+    if comm:
+        greet(place)
+    load_after = pltpu.make_async_copy(after_hbm, after, lsem.at[0])
+    load_cot = pltpu.make_async_copy(cot_hbm, gm, lsem.at[1])
+    load_after.start()
+    load_cot.start()
+
+    def fetch_fc(j):
+        return pltpu.make_async_copy(wfc_hbm.at[:, pl.ds(j * CH, CH)], wfc.at[j % 2], wsem.at[j % 2, 0])
+
+    def fetch_down(i):
+        j = i % (FF // CH)
+        return pltpu.make_async_copy(wdn_hbm.at[pl.ds(j * CH, CH), :], wdn.at[i % 2], wsem.at[i % 2, 1])
+
+    fetch_fc(0).start()
+    fetch_down(0).start()
+    load_after.wait()
+    load_cot.wait()
+
+    @pl.loop(0, D // 128)
+    def _(i):
+        rows = pl.ds(pl.multiple_of(i * 128, 128), 128)
+        xhat, _ = norm_stats(after[rows, :])
+        v = (xhat * vec_ref[1:2, :] + vec_ref[6:7, :]).astype(jnp.bfloat16)
+        n2[rows, :] = v
+        n2t[:, rows] = v.T
+        g = gm[rows, :].astype(jnp.float32) * mask_ref[rows, :]
+        gm[rows, :] = g.astype(jnp.bfloat16)
+        fin[rows, :] = jnp.zeros((128, D), jnp.float32)
+        gn2[rows, :] = jnp.zeros((128, D), jnp.float32)
+
+    n = FF // CH
+
+    def store(j):
+        return pltpu.make_async_copy(stage.at[j % 2], gdown_hbm.at[pl.ds(j * CH, CH), :], ssem.at[j % 2])
+
+    pieces = []
+    if comm:
+        bufs = rest
+        for j in range(n):
+            def put(value, j=j):
+                gfc_ref[:, pl.ds(j * CH, CH)] = value
+
+            pieces.append(Scatter(place, slots.at[j], [b.at[j] for b in bufs[:4]],
+                                  GATHER_ORDER[j % 6], bufs[4].at[j], bufs[5].at[j], put))
+
+    def advance(step, first, last):
+        if comm:
+            for now in range(first, last):
+                @pl.when(step == now)
+                def _(now=now):
+                    for stage_no in (4, 3, 2, 1, 0):
+                        j = now - DELAY[stage_no]
+                        if 0 <= j < n:
+                            pieces[j].tick(stage_no)
+                            if stage_no == 4:
+                                pieces[j].finish()
+
+    @pl.loop(0, n)
+    def _(j):
+        s = j % 2
+        fetch_fc(j).wait()
+        fetch_down(j).wait()
+        fetch_down(j + 1).start()
+
+        @pl.when(j + 1 < n)
+        def _():
+            fetch_fc(j + 1).start()
+
+        cols = pl.ds(pl.multiple_of(j * CH, CH), CH)
+        pre = dot_nn(n2[...], wfc[s]) + fcb_ref[:, cols]
+        act, slope = gelu_both(pre)
+        grad = (dot_nt(gm[...], wdn[s]) * slope).astype(jnp.bfloat16)
+        gelu[:, cols] = act
+        gp[...] = grad
+        gfcb_ref[:, cols] = jnp.sum(grad.astype(jnp.float32), axis=0, keepdims=True)
+        gn2[...] += dot_nt(gp[...], wfc[s])
+        slots[j] = dot_nn(n2t[...], gp[...]).astype(jnp.bfloat16).reshape(2, 2, 4, 2, 32, CH)
+        advance(j, 0, n)
+
+    @pl.loop(0, n)
+    def _(j):
+        s = j % 2
+        fetch_down(j + n).wait()
+
+        @pl.when(j + 1 < n)
+        def _():
+            fetch_down(j + n + 1).start()
+
+        @pl.when(j >= 2)
+        def _():
+            store(j - 2).wait()
+
+        cols = pl.ds(pl.multiple_of(j * CH, CH), CH)
+        fin[...] += dot_nn(gelu[:, cols], wdn[s])
+        stage[s] = dot_tn(gelu[:, cols], gm[...]).astype(jnp.bfloat16)
+        store(j).start()
+        advance(j + n, n, 2 * n)
+
+    store(n - 2).wait()
+    store(n - 1).wait()
+
+    def norm_step(i, sums):
+        rows = pl.ds(pl.multiple_of(i * 128, 128), 128)
+        xhat, rstd = norm_stats(after[rows, :])
+        keep = mask_ref[rows, :]
+        out_ref[rows, :] = ((after[rows, :] + fin[rows, :] + vec_ref[7:8, :]) * keep).astype(jnp.bfloat16)
+        g = gn2[rows, :]
+        y = g * vec_ref[1:2, :]
+        m1 = jnp.mean(y, axis=-1, keepdims=True)
+        m2 = jnp.mean(y * xhat, axis=-1, keepdims=True)
+        gmf = gm[rows, :].astype(jnp.float32)
+        ga = gmf + rstd * (y - m1 - xhat * m2)
+        fin[rows, :] = ga
+        gattn = ga.astype(jnp.bfloat16).astype(jnp.float32)
+        return tuple(s + jnp.sum(v, axis=0, keepdims=True)
+                     for s, v in zip(sums, (g * xhat, g, gmf, gattn)))
+
+    def half(h):
+        return pltpu.make_async_copy(fin.at[pl.ds(h * 512, 512), :], gafter_hbm.at[pl.ds(h * 512, 512), :], lsem.at[h])
+
+    zero = jnp.zeros((1, D), jnp.float32)
+    sums = lax.fori_loop(0, D // 256, norm_step, (zero,) * 4)
+    half(0).start()
+    sums = lax.fori_loop(D // 256, D // 128, norm_step, sums)
+    half(1).start()
+    for i in range(4):
+        small_ref[i:i + 1, :] = sums[i]
+    half(0).wait()
+    half(1).wait()
+
+
+def mlp(comm, after, cot, mask, vecs, fcb, wfc, wdn):
+    n = FF // CH
+    any_ = pl.BlockSpec(memory_space=pl.ANY)
+    vmem = pl.BlockSpec(memory_space=pltpu.VMEM)
+    return pl.pallas_call(
+        functools.partial(mlp_kernel, comm),
+        out_shape=[jax.ShapeDtypeStruct((D, D), jnp.bfloat16), jax.ShapeDtypeStruct((D, D), jnp.float32),
+                   jax.ShapeDtypeStruct((FF, D), jnp.bfloat16), jax.ShapeDtypeStruct((32, FF), jnp.float32),
+                   jax.ShapeDtypeStruct((8, D), jnp.float32), jax.ShapeDtypeStruct((1, FF), jnp.float32)],
+        in_specs=[any_, any_, vmem, vmem, vmem, any_, any_],
+        out_specs=[vmem, any_, any_, vmem, vmem, vmem],
+        scratch_shapes=[pltpu.VMEM((D, D), jnp.float32), pltpu.VMEM((D, D), jnp.bfloat16),
+                        pltpu.VMEM((D, D), jnp.bfloat16), pltpu.VMEM((D, D), jnp.bfloat16),
+                        pltpu.VMEM((D, FF), jnp.bfloat16), pltpu.VMEM((D, CH), jnp.bfloat16),
+                        pltpu.VMEM((D, D), jnp.float32), pltpu.VMEM((D, D), jnp.float32),
+                        pltpu.VMEM((2, D, CH), jnp.bfloat16), pltpu.VMEM((2, CH, D), jnp.bfloat16),
+                        pltpu.VMEM((2, CH, D), jnp.bfloat16),
+                        pltpu.VMEM((n, 2, 2, 4, 2, 32, CH), jnp.bfloat16),
+                        pltpu.SemaphoreType.DMA((2,)), pltpu.SemaphoreType.DMA((2, 2)), pltpu.SemaphoreType.DMA((2,))]
+        + (scatter_bufs(n, 32, CH) if comm else []),
+        compiler_params=pltpu.CompilerParams(vmem_limit_bytes=60 << 20,
+            **(dict(collective_id=2, has_side_effects=True) if comm else {})),
+    )(after, cot, mask, vecs, fcb, wfc, wdn)
+
+
 HEADS = 16
 BLOCK = 128
 
@@ -484,9 +678,9 @@
     return (*mats, *unpack_small(fulls[0].reshape(32, 16, 128)))
 
 
-def scatter_all(g_qkv, g_out, g_fc, g_down, gains, biases, fc_bias):
+def scatter_all(g_qkv, g_out, g_down, gains, biases, fc_bias):
     small = pack_small(gains, biases, fc_bias, 8, jnp.float32)
-    full = [g.astype(jnp.bfloat16) for g in (g_qkv, g_out, g_fc, g_down)]
+    full = [g.astype(jnp.bfloat16) for g in (g_qkv, g_out, g_down)]
     shapes = [(g.shape[0] // 32, g.shape[1]) for g in full]
     cuts = [
         (n, (r0, 32), (c0, 512))
@@ -494,10 +688,10 @@
         for r0 in range(0, rows, 32)
         for c0 in range(0, cols, 512)
     ]
-    count, depth = len(cuts), 18
+    count, depth = len(cuts), 16
 
     def kernel(*refs):
-        ins, outs, (slots, own, load_sem), rest = refs[:5], refs[5:10], refs[10:13], refs[13:]
+        ins, outs, (slots, own, load_sem), rest = refs[:4], refs[4:8], refs[8:11], refs[11:]
         big, little = rest[:6], rest[6:]
         place = Place()
         greet(place)
@@ -545,8 +739,8 @@
     out = pl.pallas_call(
         kernel,
         out_shape=[jax.ShapeDtypeStruct(s, jnp.float32) for s in [(8, 128)] + shapes],
-        in_specs=[pl.BlockSpec(memory_space=pl.ANY)] * 5,
-        out_specs=[pl.BlockSpec(memory_space=pltpu.VMEM)] * 5,
+        in_specs=[pl.BlockSpec(memory_space=pl.ANY)] * 4,
+        out_specs=[pl.BlockSpec(memory_space=pltpu.VMEM)] * 4,
         scratch_shapes=[pltpu.VMEM((depth, 2, 2, 4, 2, 32, 512), jnp.bfloat16),
                         pltpu.VMEM((2, 2, 4, 2, 8, 128), jnp.float32),
                         pltpu.SemaphoreType.DMA((depth + 1,))]
@@ -597,32 +791,22 @@
     mixed = jnp.einsum("bhqk,bkhd->bqhd", probs, values, preferred_element_type=jnp.float32)
     mixed = mixed.reshape(row_total, model_width).astype(jnp.bfloat16)
     after_attn = hidden + jnp.dot(mixed, full_out, preferred_element_type=jnp.float32) + bias_f[3]
-    normed_two_f, norm_back_two = jax.vjp(layer_norm, after_attn, gain_f[1], bias_f[4])
-    normed_two = normed_two_f.astype(jnp.bfloat16)
-    pre_gelu = jnp.dot(
-        normed_two, full_fc, preferred_element_type=jnp.float32
-    ) + full_fc_bias.astype(jnp.float32)
-    gelu_f, gelu_back = jax.vjp(partial(jax.nn.gelu, approximate=False), pre_gelu)
-    gelu_out = gelu_f.astype(jnp.bfloat16)
-    final_rows = (
-        after_attn + jnp.dot(gelu_out, full_down, preferred_element_type=jnp.float32) + bias_f[5]
-    )
-    output = (final_rows * keep_rows).astype(jnp.bfloat16).reshape(tokens.shape)
-    back_fc, back_down, back_qkv, back_out = full_fc, full_down, full_qkv, full_out
-    grad_final = cotangent.reshape(row_total, model_width).astype(jnp.float32) * keep_rows
-    grad_mlp = grad_final.astype(jnp.bfloat16)
-    grad_down_local = outer_sum(gelu_out, grad_mlp)
-    grad_down_bias = jnp.sum(grad_mlp.astype(jnp.float32), axis=0)
-    grad_gelu = times_transposed(grad_mlp, back_down)
-    grad_pre = gelu_back(grad_gelu)[0].astype(jnp.bfloat16)
-    grad_fc_local = outer_sum(normed_two, grad_pre)
-    grad_fc_bias_local = jnp.sum(grad_pre.astype(jnp.float32), axis=0)
-    grad_normed_two = times_transposed(grad_pre, back_fc)
-    grad_after_norm, grad_gain_two, grad_shift_two = norm_back_two(grad_normed_two)
-    grad_after = grad_final + grad_after_norm
+    vecs = jnp.concatenate([gain_f, bias_f], axis=0)
+    output, grad_after, grad_down_local, grad_w_fc, two_sums, grad_fc_bias_local = mlp(
+        True,
+        after_attn,
+        cotangent.reshape(row_total, model_width),
+        keep_rows,
+        vecs,
+        full_fc_bias.astype(jnp.float32).reshape(1, -1),
+        full_fc,
+        full_down,
+    )
+    output = output.reshape(tokens.shape)
+    grad_fc_bias_local = grad_fc_bias_local.reshape(-1)
+    back_qkv, back_out = full_qkv, full_out
     grad_attn = grad_after.astype(jnp.bfloat16)
     grad_out_local = outer_sum(mixed, grad_attn)
-    grad_out_bias = jnp.sum(grad_attn.astype(jnp.float32), axis=0)
     grad_mixed = times_transposed(grad_attn, back_out).astype(jnp.bfloat16).reshape(head_shape)
     probs_full = jnp.exp(masked_scores(queries, key_rows) - log_total)
     grad_probs = jnp.einsum(
@@ -653,19 +837,19 @@
     grad_normed = times_transposed(grad_projected, back_qkv)
     grad_hidden_norm, grad_gain_one, grad_shift_one = norm_back_one(grad_normed)
     grad_input = (grad_after + grad_hidden_norm).astype(jnp.bfloat16).reshape(tokens.shape)
-    gains_local = jnp.stack([grad_gain_one, grad_gain_two])
+    gains_local = jnp.stack([grad_gain_one, two_sums[0]])
     biases_local = jnp.stack(
         [
             grad_shift_one,
             grad_query_bias,
             grad_value_bias,
-            grad_out_bias,
-            grad_shift_two,
-            grad_down_bias,
+            two_sums[3],
+            two_sums[1],
+            two_sums[2],
         ]
     )
-    grad_w_qkv, grad_w_out, grad_w_fc, grad_w_down, grad_gains, grad_biases, grad_fc_bias = scatter_all(
-        grad_qkv_local, grad_out_local, grad_fc_local, grad_down_local,
+    grad_w_qkv, grad_w_out, grad_w_down, grad_gains, grad_biases, grad_fc_bias = scatter_all(
+        grad_qkv_local, grad_out_local, grad_down_local,
         gains_local, biases_local, grad_fc_bias_local,
     )
     return (

time: 580 us -> 503 us (0.87)
  matrix products: 181 us -> 70.2 us
  Pallas kernels: 269 us -> 326 us
  other arithmetic: 47.1 us -> 31.8 us
  local copies, waits for them, and re-layouts: 75.3 us -> 67.9 us
    pallas_call x0 -> x1, Pallas kernels: none -> 88.3 us  [mlp(): pl.pallas_call(functools.partial(mlp_kernel, comm), out_shape=[jax.ShapeD...]
    dot_general x4 -> x2, matrix products: 82.5 us -> 12 us  [times_transposed(): lax.dot_general(first, second, (((1,), (1,)), ((), ())), preferred_elemen...]
    pallas_call x1, Pallas kernels: 122 us -> 90.9 us  [scatter_all(): pl.pallas_call(kernel, out_shape=[jax.ShapeDtypeStruct(s, jnp.float32) fo...]
    dot_general x2 -> x0, matrix products: 27.1 us -> none  [the longest x1 14.8 us: body(): jnp.dot(gelu_out, full_down, preferred_element_type=jnp.float32)]
    dot_general x4 -> x2, matrix products: 39.1 us -> 15.3 us  [outer_sum(): lax.dot_general(first, second, (((0,), (0,)), ((), ())), preferred_elemen...]
    convert_element_type x4 -> x2, other arithmetic: 14.1 us -> 6.81 us  [the longest x1 5.35 us: body(): (grad_after + grad_hidden_norm).astype(jnp.bfloat16).reshape(tokens.shape)]
    unnamed x121 -> x69, local copies, waits for them, and re-layouts: 16.1 us -> 9.05 us
where the time goes in v2:
time: 503 us; the launch traced here: 497 us
  Pallas kernels  326 us (65%)
  matrix products  70.2 us (14%)
  local copies, waits for them, and re-layouts  67.9 us (13%)
  other arithmetic  31.8 us (6%)
    pallas_call x1, Pallas kernels, gather_all(): pl.pallas_call(kernel, out_shape=[jax.ShapeDtypeStruct((2, 2, 4, 2) + s.s...  146 us
    pallas_call x1, Pallas kernels, scatter_all(): pl.pallas_call(kernel, out_shape=[jax.ShapeDtypeStruct(s, jnp.float32) fo...  90.9 us
    pallas_call x1, Pallas kernels, mlp(): pl.pallas_call(functools.partial(mlp_kernel, comm), out_shape=[jax.ShapeD...  88.3 us
    dot_general x2, matrix products, outer_sum(): lax.dot_general(first, second, (((0,), (0,)), ((), ())), preferred_elemen...  15.3 us
    reshape x2, local copies, waits for them, and re-layouts, body(): times_transposed(grad_attn, back_out).astype(jnp.bfloat16)  12.4 us
    dot_general x2, matrix products, times_transposed(): lax.dot_general(first, second, (((1,), (1,)), ((), ())), preferred_elemen...  12 us

profile of v2, /device:TPU:0, one launch (start us, length us, event | category | flops | bytes accessed | tf_op | source)
XLA Modules:
  0.0 497.0 jit_solution(11583981654718963685)
XLA Ops:
  2.8 146.3 %shard_map.178 = (bf16[2,2,4,2,16,128]{5,4,3,2,1,0:T(8,128)(2,1)}, bf16[2,2,4,2,32,3072]{5,4,3,2,1,0:T(8,128)(2,1)}, bf16[2,2,4,2,32,1024]{5,4,3,2,1,0:T(8,128)(...) custom-call(bf16[16,128]{1,0:T(8,128)(2,1)} %fusion.24.refs_0_, bf16[32,3072]{1,0:T(8,128)(2,1)} %refs_1_.1, ...), custom_call_target="tpu_custom_call" | custom-call | tf_op jit(solution)/shard_map/pallas_call | solution.py:665
  157.4 9.0 %fusion.31 = f32[1024,3072]{1,0:T(8,128)} fusion(bf16[1024,1024]{1,0:T(8,128)(2,1)S(1)} %bitcast.122, bf16[1024,3072]{1,0:T(8,128)(2,1)S(1)} %bitcast.145), kind=kOutput, calls=%fused_computation.84 | convolution fusion | flops 6442450944 | bytes 20971520 | tf_op jit(solution)/shard_map/dot_general | solution.py:783
  166.5 6.1 %fusion.1 = (bf16[1024,1024]{1,0:T(8,128)(2,1)S(1)}, bf16[1024,1024]{1,0:T(8,128)(2,1)}) fusion(f32[1024,3072]{1,0:T(8,128)} %fusion.31, f32[1024]{0:T(1024)S(1)} %add.99, f32[1024]{0:T(1024)S(1)} %add.96), kind=kLoop, calls=%fused_computation.11 | loop fusion | flops 4194304 | bytes 12591104 | tf_op jit(solution)/shard_map/convert_element_type | solution.py:784
  172.6 4.0 reshape.248
  176.6 5.8 %copy.38 = bf16[8,128,16,64]{1,3,2,0:T(8,128)(2,1)} copy(bf16[8,128,16,64]{3,2,1,0:T(8,128)(2,1)} %reshape.248) | data formatting | bytes 4194304 | tf_op jit(solution)/shard_map/reshape | solution.py:784
  184.9 4.0 reshape.249
  188.9 4.9 copy.39
  193.9 4.1 fusion.30
  201.6 4.0 reshape.247
  205.6 5.1 %copy.40 = bf16[8,128,16,64]{1,3,2,0:T(8,128)(2,1)S(1)} copy(bf16[8,128,16,64]{3,2,1,0:T(8,128)(2,1)} %reshape.247) | data formatting | bytes 4194304 | tf_op jit(solution)/shard_map/reshape | solution.py:786
  210.8 4.6 convert_bitcast_fusion
  218.6 7.8 %fusion.3.after_hbm = f32[1024,1024]{1,0:T(8,128)} fusion(f32[4,256,1024]{2,1,0:T(8,128)} %get-tuple-element.54, f32[1024]{0:T(1024)S(1)} %add.104, bf16[1024,1024]{1,0:T(8,128)(2,1)} %bitcast.149, bf16[128,8,8,128]{3,2,1,0:T(8,128)(2,1)} %bitcast.125), kind=kOutput, calls=%fused_computation.16 | convolution fusion | flops 2149580800 | bytes 12587008 | tf_op jit(solution)/shard_map/dot_general | solution.py:793
  229.8 88.3 %shard_map.179 = (bf16[1024,1024]{1,0:T(8,128)(2,1)}, f32[1024,1024]{1,0:T(8,128)}, bf16[4096,1024]{1,0:T(8,128)(2,1)}, f32[32,4096]{1,0:T(8,128)}, f32[8,1024]{1,0:T(8,128)}, /*index=5*/f32[1,4096]{1,0:T(1,128)}) custom-call(f32[1024,1024]{1,0:T(8,128)} %fusion.3.after_hbm, bf16[1024,1024]{1,0:T(8,128)(2,1)} %bitcast.120, f32[1024,1]{1,0:T(8,128)} %bitcast.123, ...), custom_call_target="tpu_custom_call" | custom-call | tf_op jit(solution)/shard_map/pallas_call | solution.py:419
  318.1 6.6 %fusion.8 = bf16[1024,1024]{1,0:T(8,128)(2,1)} fusion(bf16[128,8,8,128]{3,2,1,0:T(8,128)(2,1)} %bitcast.126, f32[1024,1024]{1,0:T(8,128)} %get-tuple-element.30), kind=kOutput, calls=%fused_computation.36 | convolution fusion | flops 2149580800 | bytes 8388608 | tf_op jit(solution)/shard_map/dot_general | solution.py:452
  324.7 3.7 convolution_convert_fusion.2
  328.4 6.4 %reshape.250 = bf16[8,128,16,64]{3,2,1,0:T(8,128)(2,1)} reshape(bf16[1024,1024]{1,0:T(8,128)(2,1)} %convolution_convert_fusion.2) | data formatting | bytes 4194304 | tf_op jit(solution)/shard_map/reshape | solution.py:810
  334.8 5.9 %copy.47 = bf16[8,128,16,64]{1,3,2,0:T(8,128)(2,1)} copy(bf16[8,128,16,64]{3,2,1,0:T(8,128)(2,1)} %reshape.250) | data formatting | bytes 4194304 | tf_op jit(solution)/shard_map/reshape | solution.py:810
  340.7 7.1 %convert_reduce_fusion = (f32[16,64]{1,0:T(8,128)S(1)}, bf16[8,16,64,128]{3,2,1,0:T(8,128)(2,1)S(1)}) fusion(bf16[8,128,16,64]{1,3,2,0:T(8,128)(2,1)} %copy.47, f32[8,16,128,128]{2,3,1,0:T(8,128)} %copy-done, f32[8,16,128]{2,1,0:T(8,128)S(1)} %log_add_fusion), kind=kOutput, calls=%fused_computation.18 | convolution fusion | flops 275774464 | bytes 12652544 | tf_op jit(solution)/shard_map/bhqk,bqhd->bkhd/dot_general | solution.py:815
  351.0 5.9 %multiply_reduce_fusion = (f32[8,16,128]{2,1,0:T(8,128)S(1)}, f32[8,16,128,128]{2,3,1,0:T(8,128)S(1)}) fusion(f32[8,16,128,128]{2,3,1,0:T(8,128)} %copy-done, f32[8,16,128]{2,1,0:T(8,128)S(1)} %log_add_fusion, bf16[8,128,16,64]{1,3,2,0:T(8,128)(2,1)S(1)} %copy-done.3, bf16[8,128,16,64]{1,3,2,0:T(8,128)(2,1)S(1)} %copy.40), kind=kOutput, calls=%fused_computation.1 | convolution fusion | flops 274710528 | bytes 21102592 | tf_op jit(solution)/shard_map/bqhd,bkhd->bhqk/dot_general | solution.py:812
  370.7 8.3 %multiply_reduce_fusion.1 = (f32[1024]{0:T(1024)S(1)}, f32[1024]{0:T(1024)S(1)}, f32[1024]{0:T(1024)S(1)}, f32[1024,1024]{1,0:T(8,128)S(1)}) fusion(f32[4,256,1024]{2,1,0:T(8,128)S(1)} %copy-done.4, f32[1024]{0:T(1024)S(1)} %bitcast.136, f32[1024]{0:T(1024)S(1)} %rsqrt.14, f32[1024]{0:T(1024)S(1)} %mul.90, ...), kind=kOutput, calls=%fused_computation.20 | convolution fusion | flops 6450836480 | bytes 20996096 | tf_op jit(solution)/shard_map/dot_general | solution.py:458
  379.0 3.7 fusion.29
  382.7 8.7 %convolution_convert_fusion = bf16[1024,3072]{1,0:T(8,128)(2,1)} fusion(bf16[1024,1024]{1,0:T(8,128)(2,1)S(1)} %get-tuple-element.52, bf16[1024,3072]{0,1:T(8,128)(2,1)S(1)} %bitcast_dynamic-update-slice_fusion), kind=kOutput, calls=%fused_computation.8 | convolution fusion | flops 6445596672 | bytes 14680064 | tf_op jit(solution)/shard_map/dot_general | solution.py:452
  392.8 90.9 %shard_map.180 = (f32[8,128]{1,0:T(8,128)}, f32[32,3072]{1,0:T(8,128)}, f32[32,1024]{1,0:T(8,128)}, f32[128,1024]{1,0:T(8,128)}) custom-call(f32[2,2,4,2,8,128]{5,4,3,2,1,0:T(8,128)} %bitcast.128, bf16[2,2,4,2,32,3072]{5,4,3,2,1,0:T(8,128)(2,1)} %bitcast.119, bf16[2,2,4,2,32,1024]{5,4,3,2,1,0:T(8,128)(2,1)} %bitcast.127, ...), custom_call_target="tpu_custom_call" | custom-call | tf_op jit(solution)/shard_map/pallas_call | solution.py:739
  486.9 5.3 %add_convert_fusion.1 = bf16[1024,1024]{1,0:T(8,128)(2,1)} fusion(f32[1024,1024]{1,0:T(8,128)} %get-tuple-element.30, f32[1024,1024]{1,0:T(8,128)} %get-tuple-element.49, f32[1024]{0:T(1024)S(1)} %negate_multiply_fusion), kind=kLoop, calls=%fused_computation.21 | loop fusion | flops 3145728 | bytes 10489856 | tf_op jit(solution)/shard_map/convert_element_type | solution.py:839
  (129 shorter events, 48.7 us)
Async XLA Ops:
  0.6 152.9 %copy-start.1 = (bf16[4,256,1024]{2,1,0:T(8,128)(2,1)S(1)}, bf16[4,256,1024]{2,1,0:T(8,128)(2,1)}, u32[]{:S(2)}) copy-start(bf16[4,256,1024]{2,1,0:T(8,128)(2,1)} %param.12) | copy-start | bytes 6291460
  150.6 3.0 copy-start.2
  153.6 3.8 slice-start.2
  154.5 2.9 slice-start.3
  193.9 4.2 copy-start.5
  198.0 3.5 copy-start
  198.1 3.6 copy-start.9
  218.6 10.2 %copy-start.18 = (s32[4,256]{1,0:T(4,128)S(1)}, s32[4,256]{1,0:T(4,128)}, u32[]{:S(2)}) copy-start(s32[4,256]{1,0:T(4,128)} %param.13) | copy-start | bytes 12292
  318.1 6.6 %copy-start.10 = (f32[1024,1024]{1,0:T(8,128)S(1)}, f32[1024,1024]{1,0:T(8,128)}, u32[]{:S(2)}) copy-start(f32[1024,1024]{1,0:T(8,128)} %get-tuple-element.30) | copy-start | bytes 12582916
  318.1 6.6 %copy-start.19 = (bf16[2,2,4,2,32,1024]{5,4,3,2,1,0:T(8,128)(2,1)S(1)}, bf16[2,2,4,2,32,1024]{5,4,3,2,1,0:T(8,128)(2,1)}, u32[]{:S(2)}) copy-start(bf16[2,2,4,2,32,1024]{5,4,3,2,1,0:T(8,128)(2,1)} %get-tuple-element.26) | copy-start | bytes 6291460
  347.8 3.1 copy-start.3
  351.0 5.9 %slice-start = ((s8[8388608]{0:T(1024)(128)(4,1)}), s8[4194304]{0:T(1024)(128)(4,1)S(1)}, s32[]{:S(2)}) async-start(s8[8388608]{0:T(1024)(128)(4,1)} %bitcast.109), calls=%async_computation | async-start | bytes 8388608
  351.0 5.9 %slice-start.1 = ((s8[8388608]{0:T(1024)(128)(4,1)}), s8[4194304]{0:T(1024)(128)(4,1)S(1)}, s32[]{:S(2)}) async-start(s8[8388608]{0:T(1024)(128)(4,1)} %bitcast.109), calls=%async_computation.1 | async-start | bytes 8388608
  356.9 2.8 copy-start.7
  362.7 1.8 copy-start.6
  362.7 7.3 %slice-start.4 = ((s8[6291456]{0:T(1024)(128)(4,1)}), s8[4194304]{0:T(1024)(128)(4,1)S(1)}, s32[]{:S(2)}) async-start(s8[6291456]{0:T(1024)(128)(4,1)} %bitcast.146), calls=%async_computation.4 | async-start | bytes 8388608
  366.0 4.0 slice-start.5
  368.4 2.3 copy-start.4
  382.6 8.8 %copy-start.17 = (f32[8,1024]{1,0:T(8,128)S(1)}, f32[8,1024]{1,0:T(8,128)}, u32[]{:S(2)}) copy-start(f32[8,1024]{1,0:T(8,128)} %get-tuple-element.31) | copy-start | bytes 98308
  382.6 9.5 %copy-start.16 = (f32[1,4096]{1,0:T(1,128)S(1)}, f32[1,4096]{1,0:T(1,128)}, u32[]{:S(2)}) copy-start(f32[1,4096]{1,0:T(1,128)} %get-tuple-element.32) | copy-start | bytes 49156
  486.9 5.4 %copy-start.11 = (bf16[1024,1024]{1,0:T(8,128)(2,1)S(1)}, bf16[1024,1024]{1,0:T(8,128)(2,1)}, u32[]{:S(2)}) copy-start(bf16[1024,1024]{1,0:T(8,128)(2,1)} %get-tuple-element.29) | copy-start | bytes 6291460
  492.3 2.1 copy-start.15
  492.3 2.7 copy-start.12
  492.3 3.5 copy-start.13
  (2 other events, 2.9 us)

commit v3 on v2

--- a/solution.py
+++ b/solution.py
@@ -137,12 +137,14 @@
             guarded(cond, end)
 
 
-def run_ticks(pieces, starts):
+def run_ticks(pieces, starts, between=None):
     last = max(s + len(p.ticks) for p, s in zip(pieces, starts))
     for now in range(last):
         for p, s in zip(pieces, starts):
             if 0 <= now - s < len(p.ticks):
                 p.tick(now - s)
+        if between and now in between:
+            between[now]()
     for p in pieces:
         p.finish()
 
@@ -470,6 +472,366 @@
     return jnp.where(causal, scores, -1e30)
 
 
+def lane_low(shape):
+    return lax.broadcasted_iota(jnp.int32, shape, len(shape) - 1) < 64
+
+
+def stack_heads(pair):
+    low = lane_low(pair.shape)
+    zero = jnp.zeros_like(pair)
+    return jnp.concatenate([jnp.where(low, pair, zero), jnp.where(low, zero, pair)], axis=0)
+
+
+def merge_heads(stacked):
+    half = stacked.shape[0] // 2
+    return jnp.where(lane_low((half, stacked.shape[1])), stacked[:half], stacked[half:])
+
+
+def softmax_pair(query2, key2):
+    scores = dot_nt(query2, key2) * 0.125
+    row = lax.broadcasted_iota(jnp.int32, scores.shape, 0) % BLOCK
+    col = lax.broadcasted_iota(jnp.int32, scores.shape, 1)
+    scores = jnp.where(row >= col, scores, -1e30)
+    top = jnp.max(scores, axis=-1, keepdims=True)
+    raised = jnp.exp(scores - top)
+    return raised * (1.0 / jnp.sum(raised, axis=-1, keepdims=True))
+
+
+GATHER_CUTS = ([(0, (0, 16), (0, 128))]
+               + [(1, (0, 32), (i * 512, 512)) for i in range(6)]
+               + [(2, (0, 32), (i * 512, 512)) for i in range(2)]
+               + [(3, (0, 32), (i * 512, 512)) for i in range(8)]
+               + [(4, (i * 16, 16), (0, 1024)) for i in range(8)])
+
+
+def gather_kernel(small, wqkv_s, wout_s, wfc_s, wdn_s, tok_hbm, cond_hbm,
+                  small_f, wqkv_f, wout_f, wfc_f, wdn_f, qkv_hbm, mixed_hbm, after_hbm, vec_ref, fcb_ref,
+                  tok, cond, hidden, normed, wqkv, wout, qkv, mixed, smallv,
+                  send, recv, own_sem, lsem, wsem, osem):
+    ins = (small, wqkv_s, wout_s, wfc_s, wdn_s)
+    fulls = (small_f, wqkv_f, wout_f, wfc_f, wdn_f)
+    place = Place()
+    greet(place)
+    own = [pltpu.make_async_copy(s, f.at[place.y, place.x, place.z, place.c], own_sem.at[i])
+           for i, (s, f) in enumerate(zip(ins, fulls))]
+    loads = [pltpu.make_async_copy(tok_hbm, tok, lsem.at[0]), pltpu.make_async_copy(cond_hbm, cond, lsem.at[1])]
+    for c in own + loads:
+        c.start()
+    for c in own:
+        c.wait()
+
+    def make(k):
+        n, (r0, r), (c0, w) = GATHER_CUTS[k]
+        view = lambda y, x, z, c: fulls[n].at[y, x, z, c, pl.ds(r0, r), pl.ds(c0, w)]
+        return Gather(place, view, GATHER_ORDER[k % 6], send.at[k], recv.at[k], 1)
+
+    load_small = pltpu.make_async_copy(small_f, smallv, lsem.at[2])
+    load_qkv = pltpu.make_async_copy(wqkv_f, wqkv, wsem.at[0])
+    load_out = pltpu.make_async_copy(wout_f, wout, wsem.at[1])
+    store_qkv = pltpu.make_async_copy(qkv, qkv_hbm, osem.at[0])
+    store_mixed = pltpu.make_async_copy(mixed, mixed_hbm, osem.at[1])
+    store_after = pltpu.make_async_copy(hidden, after_hbm, osem.at[2])
+
+    def add_hidden():
+        for c in loads:
+            c.wait()
+
+        @pl.loop(0, D // 128)
+        def _(i):
+            rows = pl.ds(pl.multiple_of(i * 128, 128), 128)
+            hidden[rows, :] = tok[rows, :].astype(jnp.float32) + cond[rows, :].astype(jnp.float32)
+
+    def first_norm():
+        load_small.start()
+        load_small.wait()
+        for g in range(8):
+            win, z0 = g // 2, (g % 2) * 2
+            total = None
+            for i in range(4):
+                y, x, z, c = win // 2, win % 2, z0 + i // 2, i % 2
+                one = smallv[y, x, z, c].astype(jnp.float32)
+                device = g * 4 + i
+                fcb_ref[:, device * 128:(device + 1) * 128] = one[8:9]
+                total = one[:8] if total is None else total + one[:8]
+            vec_ref[:, g * 128:(g + 1) * 128] = total
+
+        @pl.loop(0, D // 128)
+        def _(i):
+            rows = pl.ds(pl.multiple_of(i * 128, 128), 128)
+            xhat, _ = norm_stats(hidden[rows, :])
+            normed[rows, :] = (xhat * vec_ref[0:1, :] + vec_ref[2:3, :]).astype(jnp.bfloat16)
+
+    def project(first, last):
+        for i in range(first, last):
+            cols = slice(i * 512, (i + 1) * 512)
+            weight = wqkv[:, :, :, :, :, cols].reshape(D, 512)
+            part = dot_nn(normed[...], weight)
+            if i < 2:
+                part = part + vec_ref[3:4, cols]
+            if i >= 4:
+                part = part + vec_ref[4:5, i * 512 - 2048:i * 512 - 1536]
+            qkv[:, cols] = part.astype(jnp.bfloat16)
+
+    def attend(first, last):
+        @pl.loop(first, last)
+        def _(b):
+            rows = pl.ds(pl.multiple_of(b * BLOCK, BLOCK), BLOCK)
+            for pair in range(8):
+                q2 = stack_heads(qkv[rows, pair * 128:(pair + 1) * 128])
+                k2 = qkv[rows, 1024 + pair * 128:1024 + (pair + 1) * 128]
+                v2 = qkv[rows, 2048 + pair * 128:2048 + (pair + 1) * 128]
+                probs = softmax_pair(q2, k2).astype(jnp.bfloat16)
+                mixed[rows, pair * 128:(pair + 1) * 128] = merge_heads(dot_nn(probs, v2)).astype(jnp.bfloat16)
+
+    def output_projection():
+        load_out.wait()
+        for i in range(2):
+            cols = slice(i * 512, (i + 1) * 512)
+            part = dot_nn(mixed[...], wout[:, :, :, :, :, cols].reshape(D, 512))
+            hidden[:, cols] += part + vec_ref[5:6, cols]
+        store_after.start()
+
+    def step8():
+        load_qkv.wait()
+        project(0, 6)
+        store_qkv.start()
+
+    def step7():
+        load_qkv.start()
+
+    def step9():
+        load_out.start()
+        attend(0, 4)
+
+    def step10():
+        attend(4, 8)
+        store_mixed.start()
+
+    between = {0: add_hidden, 5: first_norm, 7: step7, 8: step8, 9: step9, 10: step10, 11: output_projection}
+    run_ticks([make(k) for k in range(len(GATHER_CUTS))], [(k + 2) // 3 for k in range(len(GATHER_CUTS))], between)
+    store_qkv.wait()
+    store_mixed.wait()
+    store_after.wait()
+
+
+def gather_and_attend(shards, tok, cond):
+    any_ = pl.BlockSpec(memory_space=pl.ANY)
+    vmem = pl.BlockSpec(memory_space=pltpu.VMEM)
+    count = len(GATHER_CUTS)
+    bf, f32 = jnp.bfloat16, jnp.float32
+    dma = pltpu.SemaphoreType.DMA
+    return pl.pallas_call(
+        gather_kernel,
+        out_shape=[jax.ShapeDtypeStruct((2, 2, 4, 2) + s.shape, s.dtype) for s in shards]
+        + [jax.ShapeDtypeStruct((D, 3 * D), bf), jax.ShapeDtypeStruct((D, D), bf), jax.ShapeDtypeStruct((D, D), f32),
+           jax.ShapeDtypeStruct((8, D), f32), jax.ShapeDtypeStruct((1, FF), f32)],
+        in_specs=[any_] * 7,
+        out_specs=[any_] * 8 + [vmem] * 2,
+        scratch_shapes=[pltpu.VMEM((D, D), bf), pltpu.VMEM((D, D), bf), pltpu.VMEM((D, D), f32), pltpu.VMEM((D, D), bf),
+                        pltpu.VMEM((2, 2, 4, 2, 32, 3 * D), bf), pltpu.VMEM((2, 2, 4, 2, 32, D), bf),
+                        pltpu.VMEM((D, 3 * D), bf), pltpu.VMEM((D, D), bf), pltpu.VMEM((2, 2, 4, 2, 16, 128), bf),
+                        dma((count, GATHER_SEMS)), dma((count, GATHER_SEMS)), dma((5,)), dma((3,)), dma((2,)), dma((3,))],
+        compiler_params=pltpu.CompilerParams(collective_id=0, has_side_effects=True, vmem_limit_bytes=60 << 20),
+    )(*shards, tok, cond)
+
+
+def own_small(gains, biases, fc_bias):
+    seq = lax.axis_index("seq")
+    eight = jnp.concatenate([gains, biases], axis=0)
+    placed = jnp.where(jnp.arange(4)[None, :, None] == seq % 4, eight[:, None, :], 0).reshape(8, 128)
+    return jnp.concatenate([placed, fc_bias.reshape(1, 128), jnp.zeros((7, 128), fc_bias.dtype)], axis=0)
+
+
+DOWN_CUTS = [(r0, c0) for r0 in range(0, 128, 32) for c0 in (0, 512)]
+OFFSETS = (0, 1, 3, 4, 6)
+DOWN_START = (0, 0, 1, 2, 3, 4, 5, 6)
+
+
+def backward_kernel(gafter_hbm, qkv_hbm, mixed_hbm, tok_hbm, cond_hbm, wqkv_hbm, wout_hbm, gdown_hbm, vec_ref,
+                    sums_ref, fcb_ref,
+                    gin_hbm, gqkv_ref, gout_ref, gdown_ref, small_ref,
+                    gafter, gattn, mixed, qkv, gqkv, tok, cond, normed, slots, own, lsem, dsem,
+                    *rest):
+    big, little = rest[:6], rest[6:]
+    place = Place()
+    greet(place)
+    loads = [pltpu.make_async_copy(s, d, lsem.at[i]) for i, (s, d) in enumerate((
+        (gafter_hbm, gafter), (mixed_hbm, mixed), (wout_hbm, normed), (tok_hbm, tok), (cond_hbm, cond), (qkv_hbm, qkv)))]
+    down_loads = [pltpu.make_async_copy(gdown_hbm.at[:, :, :, :, pl.ds(r0, 32), pl.ds(c0, 512)], slots.at[i], dsem.at[i])
+                  for i, (r0, c0) in enumerate(DOWN_CUTS)]
+    for c in down_loads[:2] + loads + down_loads[2:]:
+        c.start()
+    load_wqkv = pltpu.make_async_copy(wqkv_hbm, qkv, lsem.at[6])
+
+    def piece(k, slot, put):
+        return Scatter(place, slots.at[slot], [b.at[k] for b in big[:4]], GATHER_ORDER[k % 6],
+                       big[4].at[k], big[5].at[k], put)
+
+    def putter(ref, r0, c0):
+        def put(value):
+            ref[pl.ds(r0, 32), pl.ds(c0, 512)] = value
+        return put
+
+    agenda = []
+    for i, (r0, c0) in enumerate(DOWN_CUTS):
+        agenda.append((piece(i, i, putter(gdown_ref, r0, c0)), [DOWN_START[i] + o for o in OFFSETS]))
+    for i in range(2):
+        agenda.append((piece(8 + i, 8 + i, putter(gout_ref, 0, i * 512)), [7 + i + o for o in OFFSETS]))
+    for i, ready in enumerate((7, 8, 9, 14, 15, 16)):
+        col = (i % 3) * 1024 + (i // 3) * 512
+        start = ready + (2, 2, 2, 0, 0, 0)[i]
+        agenda.append((piece(10 + i, i, putter(gqkv_ref, 0, col)), [start + o for o in LATE[i]]))
+
+    def put_small(value):
+        small_ref[...] = value
+
+    agenda.append((Scatter(place, own, [b.at[0] for b in little[:4]], 2, little[4].at[0], little[5].at[0], put_small),
+                   [SMALL_START + o for o in range(5)]))
+    last_step = max(steps[-1] for _, steps in agenda)
+
+    def grad_w_out():
+        for c in loads[:2]:
+            c.wait()
+
+        @pl.loop(0, 8)
+        def _(i):
+            rows = pl.ds(pl.multiple_of(i * 128, 128), 128)
+            gattn[rows, :] = gafter[rows, :].astype(jnp.bfloat16)
+
+        for i in range(2):
+            part = dot_tn(mixed[...], gattn[:, i * 512:(i + 1) * 512])
+            slots[8 + i] = part.astype(jnp.bfloat16).reshape(2, 2, 4, 2, 32, 512)
+
+    def grad_mixed():
+        for c in loads[2:]:
+            c.wait()
+        for i in range(2):
+            cols = slice(i * 512, (i + 1) * 512)
+            mixed[:, cols] = dot_nt(gattn[...], normed[cols, :]).astype(jnp.bfloat16)
+
+        @pl.loop(0, 8)
+        def _(i):
+            rows = pl.ds(pl.multiple_of(i * 128, 128), 128)
+            xhat, _ = norm_stats(tok[rows, :].astype(jnp.float32) + cond[rows, :].astype(jnp.float32))
+            normed[rows, :] = (xhat * vec_ref[0:1, :] + vec_ref[2:3, :]).astype(jnp.bfloat16)
+
+    def attention_back(half, first, last):
+        @pl.loop(first, last)
+        def _(b):
+            rows = pl.ds(pl.multiple_of(b * BLOCK, BLOCK), BLOCK)
+            for pair in range(half * 4, half * 4 + 4):
+                c0 = pair * 128
+                q2 = stack_heads(qkv[rows, c0:c0 + 128])
+                k2 = qkv[rows, 1024 + c0:1024 + c0 + 128]
+                v2 = qkv[rows, 2048 + c0:2048 + c0 + 128]
+                g2 = stack_heads(mixed[rows, c0:c0 + 128])
+                p32 = softmax_pair(q2, k2)
+                gprobs = dot_nt(g2, v2)
+                gvalue = dot_tn(p32.astype(jnp.bfloat16), g2)
+                spread = jnp.sum(p32 * gprobs, axis=-1, keepdims=True)
+                gscores = (p32 * (gprobs - spread)).astype(jnp.bfloat16)
+                gquery = merge_heads(dot_nn(gscores, k2)) * 0.125
+                gkey = dot_tn(gscores, q2) * 0.125
+                gqkv[rows, c0:c0 + 128] = gquery.astype(jnp.bfloat16)
+                gqkv[rows, 1024 + c0:1024 + c0 + 128] = gkey.astype(jnp.bfloat16)
+                gqkv[rows, 2048 + c0:2048 + c0 + 128] = gvalue.astype(jnp.bfloat16)
+
+    def grad_w_qkv(i):
+        col = (i % 3) * 1024 + (i // 3) * 512
+        part = dot_tn(normed[...], gqkv[:, col:col + 512])
+        slots[i] = part.astype(jnp.bfloat16).reshape(2, 2, 4, 2, 32, 512)
+
+    zero = jnp.zeros((1, D), jnp.float32)
+    totals = [zero] * 4
+
+    def input_back(h):
+        if h == 0:
+            load_wqkv.wait()
+        rows512 = pl.ds(h * 512, 512)
+        gnormed = dot_nt(gqkv[rows512, :], qkv[...])
+        gafter2 = gnormed
+
+        xhat, rstd = norm_stats(tok[rows512, :].astype(jnp.float32) + cond[rows512, :].astype(jnp.float32))
+        y = gafter2 * vec_ref[0:1, :]
+        m1 = jnp.mean(y, axis=-1, keepdims=True)
+        m2 = jnp.mean(y * xhat, axis=-1, keepdims=True)
+        normed[rows512, :] = (gafter[rows512, :] + rstd * (y - m1 - xhat * m2)).astype(jnp.bfloat16)
+        add = (jnp.sum(gafter2 * xhat, axis=0, keepdims=True), jnp.sum(gafter2, axis=0, keepdims=True),
+               jnp.sum(gqkv[rows512, :D].astype(jnp.float32), axis=0, keepdims=True),
+               jnp.sum(gqkv[rows512, 2 * D:].astype(jnp.float32), axis=0, keepdims=True))
+        for i in range(4):
+            totals[i] = totals[i] + add[i]
+        pltpu.make_async_copy(normed.at[rows512, :], gin_hbm.at[rows512, :], dsem.at[h]).start()
+
+    def fill_small():
+        gain1, shift1, qbias, vbias = totals
+        eight = jnp.concatenate([gain1, sums_ref[0:1], shift1, qbias, vbias, sums_ref[3:4], sums_ref[1:2], sums_ref[2:3]],
+                                axis=0)
+        for device in range(32):
+            g = device // 4
+            w, s = device // 8, device % 8
+            at = (w // 2, w % 2, s // 2, s % 2)
+            own[at + (slice(0, 8),)] = eight[:, g * 128:(g + 1) * 128]
+            own[at + (slice(8, 16),)] = jnp.broadcast_to(fcb_ref[:, device * 128:(device + 1) * 128], (8, 128))
+
+    work = {1: [grad_w_out], 2: [grad_mixed]}
+    for i in range(4):
+        work[3 + i] = [functools.partial(attention_back, 0, 2 * i, 2 * i + 2)]
+        work[10 + i] = [functools.partial(attention_back, 1, 2 * i, 2 * i + 2)]
+    work[13].append(load_wqkv.start)
+    for i, ready in enumerate((7, 8, 9, 14, 15, 16)):
+        work[ready] = [functools.partial(grad_w_qkv, i)]
+    work[17] = [functools.partial(input_back, 0)]
+    work[18] = [functools.partial(input_back, 1), fill_small]
+    waited = set()
+    for step in range(last_step + 1):
+        for f in work.get(step, ()):
+            f()
+        for stage_no in (4, 3, 2, 1, 0):
+            for number, (p, steps) in enumerate(agenda):
+                if steps[stage_no] == step:
+                    if stage_no == 0 and number < 8:
+                        down_loads[number].wait()
+                    p.tick(stage_no)
+                    if stage_no == 4:
+                        p.finish()
+    for h in range(2):
+        rows512 = pl.ds(h * 512, 512)
+        pltpu.make_async_copy(normed.at[rows512, :], gin_hbm.at[rows512, :], dsem.at[h]).wait()
+
+
+LATE = ((0, 1, 3, 4, 6), (0, 1, 3, 4, 6), (0, 1, 3, 4, 6), (0, 1, 3, 4, 5), (0, 1, 3, 4, 5), (0, 1, 3, 4, 5))
+SMALL_START = 18
+
+
+def backward(gafter, qkv, mixed, tok, cond, wqkv, wout, gdown, vecs, sums, fcb):
+    any_ = pl.BlockSpec(memory_space=pl.ANY)
+    vmem = pl.BlockSpec(memory_space=pltpu.VMEM)
+    bf, f32 = jnp.bfloat16, jnp.float32
+    dma = pltpu.SemaphoreType.DMA
+    return pl.pallas_call(
+        backward_kernel,
+        out_shape=[jax.ShapeDtypeStruct((D, D), bf), jax.ShapeDtypeStruct((32, 3 * D), f32),
+                   jax.ShapeDtypeStruct((32, D), f32), jax.ShapeDtypeStruct((128, D), f32),
+                   jax.ShapeDtypeStruct((16, 128), f32)],
+        in_specs=[any_] * 8 + [vmem] * 3,
+        out_specs=[any_] + [vmem] * 4,
+        scratch_shapes=[pltpu.VMEM((D, D), f32), pltpu.VMEM((D, D), bf), pltpu.VMEM((D, D), bf),
+                        pltpu.VMEM((D, 3 * D), bf), pltpu.VMEM((D, 3 * D), bf), pltpu.VMEM((D, D), bf),
+                        pltpu.VMEM((D, D), bf), pltpu.VMEM((D, D), bf),
+                        pltpu.VMEM((10, 2, 2, 4, 2, 32, 512), bf), pltpu.VMEM((2, 2, 4, 2, 16, 128), f32),
+                        dma((7,)), dma((8,))]
+        + scatter_bufs(16, 32, 512) + scatter_bufs(1, 16, 128, f32),
+        compiler_params=pltpu.CompilerParams(collective_id=1, has_side_effects=True, vmem_limit_bytes=63 << 20),
+    )(gafter, qkv, mixed, tok, cond, wqkv, wout, gdown, vecs, sums, fcb)
+
+
+def own_sums(small):
+    seq = lax.axis_index("seq")
+    mine = lax.dynamic_slice(small, (0, (seq % 4) * 32), (8, 32))
+    return mine[:2], mine[2:], small[8]
+
+
 def plain_body(
     tokens,
     condition,
@@ -618,140 +980,6 @@
 GATHER_ORDER = (2, 0, 2, 2, 1, 2)
 
 
-def pack_small(gains, biases, fc_bias, rows, dtype):
-    devices = fc_bias.shape[0] // 128
-    eight = jnp.concatenate([gains, biases], axis=0)
-    eight = eight.reshape(8, devices, 32).transpose(1, 0, 2).reshape(devices, 2, 128)
-    packed = jnp.concatenate([eight, fc_bias.reshape(devices, 1, 128)], axis=1)
-    return jnp.pad(packed, ((0, 0), (0, rows - 3), (0, 0))).astype(dtype)
-
-
-def unpack_small(packed):
-    devices = packed.shape[0]
-    eight = packed[:, :2].reshape(devices, 8, 32).transpose(1, 0, 2).reshape(8, devices * 32)
-    return eight[:2], eight[2:], packed[:, 2].reshape(devices * 128)
-
-
-def gather_all(w_qkv, w_out, w_fc, w_down, norm_gains, biases, fc_bias):
-    small = pack_small(norm_gains, biases, fc_bias, 16, jnp.bfloat16)[0]
-    shards = (small, w_qkv, w_out, w_fc, w_down)
-    cuts = [(0, (0, 16), (0, 128))]
-    cuts += [(1, (0, 32), (i * 512, 512)) for i in range(6)]
-    cuts += [(2, (0, 32), (i * 512, 512)) for i in range(2)]
-    cuts += [(3, (0, 32), (i * 512, 512)) for i in range(8)]
-    cuts += [(4, (i * 16, 16), (0, 1024)) for i in range(8)]
-    count = len(cuts)
-
-    def kernel(*refs):
-        ins, fulls, (send, recv, local) = refs[:5], refs[5:10], refs[10:]
-        place = Place()
-        greet(place)
-        own = [
-            pltpu.make_async_copy(s, f.at[place.y, place.x, place.z, place.c], local.at[i])
-            for i, (s, f) in enumerate(zip(ins, fulls))
-        ]
-        for c in own:
-            c.start()
-        for c in own:
-            c.wait()
-
-        def make(k):
-            n, (r0, r), (c0, w) = cuts[k]
-            view = lambda y, x, z, c: fulls[n].at[y, x, z, c, pl.ds(r0, r), pl.ds(c0, w)]
-            return Gather(place, view, GATHER_ORDER[k % 6], send.at[k], recv.at[k], 1)
-
-        run_ticks([make(k) for k in range(count)], [(k + 2) // 3 for k in range(count)])
-
-    fulls = pl.pallas_call(
-        kernel,
-        out_shape=[jax.ShapeDtypeStruct((2, 2, 4, 2) + s.shape, s.dtype) for s in shards],
-        in_specs=[pl.BlockSpec(memory_space=pl.ANY)] * 5,
-        out_specs=[pl.BlockSpec(memory_space=pl.ANY)] * 5,
-        scratch_shapes=[
-            pltpu.SemaphoreType.DMA((count, GATHER_SEMS)),
-            pltpu.SemaphoreType.DMA((count, GATHER_SEMS)),
-            pltpu.SemaphoreType.DMA((5,)),
-        ],
-        compiler_params=pltpu.CompilerParams(collective_id=0, has_side_effects=True),
-    )(*shards)
-    mats = [f.reshape(-1, f.shape[-1]) for f in fulls[1:]]
-    return (*mats, *unpack_small(fulls[0].reshape(32, 16, 128)))
-
-
-def scatter_all(g_qkv, g_out, g_down, gains, biases, fc_bias):
-    small = pack_small(gains, biases, fc_bias, 8, jnp.float32)
-    full = [g.astype(jnp.bfloat16) for g in (g_qkv, g_out, g_down)]
-    shapes = [(g.shape[0] // 32, g.shape[1]) for g in full]
-    cuts = [
-        (n, (r0, 32), (c0, 512))
-        for n, (rows, cols) in enumerate(shapes)
-        for r0 in range(0, rows, 32)
-        for c0 in range(0, cols, 512)
-    ]
-    count, depth = len(cuts), 16
-
-    def kernel(*refs):
-        ins, outs, (slots, own, load_sem), rest = refs[:4], refs[4:8], refs[8:11], refs[11:]
-        big, little = rest[:6], rest[6:]
-        place = Place()
-        greet(place)
-
-        def make(k):
-            n, (r0, r), (c0, w) = cuts[k]
-
-            def put(value):
-                outs[n + 1][pl.ds(r0, r), pl.ds(c0, w)] = value
-
-            return Scatter(place, slots.at[k % depth], [b.at[k] for b in big[:4]],
-                           GATHER_ORDER[k % 6], big[4].at[k], big[5].at[k], put)
-
-        def put_small(value):
-            outs[0][...] = value
-
-        def load(k):
-            n, (r0, r), (c0, w) = cuts[k]
-            return pltpu.make_async_copy(
-                ins[n + 1].at[:, :, :, :, pl.ds(r0, r), pl.ds(c0, w)],
-                slots.at[k % depth], load_sem.at[k % depth])
-
-        small_load = pltpu.make_async_copy(ins[0], own, load_sem.at[depth])
-        small_load.start()
-        pieces = [Scatter(place, own, [b.at[0] for b in little[:4]], 2,
-                          little[4].at[0], little[5].at[0], put_small)]
-        pieces += [make(k) for k in range(count)]
-        loads = [small_load] + [load(k) for k in range(count)]
-        groups = [[0, 1, 2, 3]] + [list(range(i, min(i + 3, count + 1))) for i in range(4, count + 1, 3)]
-        for k in groups[0][1:]:
-            loads[k].start()
-        for now in range(len(groups) + 4):
-            if now + 1 < len(groups):
-                for k in groups[now + 1]:
-                    loads[k].start()
-            for age in range(4, -1, -1):
-                if 0 <= now - age < len(groups):
-                    for k in groups[now - age]:
-                        if age == 0:
-                            loads[k].wait()
-                        pieces[k].tick(age)
-                        if age == 4:
-                            pieces[k].finish()
-
-    out = pl.pallas_call(
-        kernel,
-        out_shape=[jax.ShapeDtypeStruct(s, jnp.float32) for s in [(8, 128)] + shapes],
-        in_specs=[pl.BlockSpec(memory_space=pl.ANY)] * 4,
-        out_specs=[pl.BlockSpec(memory_space=pltpu.VMEM)] * 4,
-        scratch_shapes=[pltpu.VMEM((depth, 2, 2, 4, 2, 32, 512), jnp.bfloat16),
-                        pltpu.VMEM((2, 2, 4, 2, 8, 128), jnp.float32),
-                        pltpu.SemaphoreType.DMA((depth + 1,))]
-        + scatter_bufs(count, 32, 512) + scatter_bufs(1, 8, 128, jnp.float32),
-        compiler_params=pltpu.CompilerParams(
-            collective_id=1, has_side_effects=True, vmem_limit_bytes=60 << 20),
-    )(small.reshape(2, 2, 4, 2, 8, 128),
-      *[g.reshape((2, 2, 4, 2) + s) for g, s in zip(full, shapes)])
-    return (*out[1:], *unpack_small(out[0][None]))
-
-
 def body(
     tokens,
     condition,
@@ -765,96 +993,32 @@
     fc_bias,
     cotangent,
 ):
-    window_count, span_rows, model_width = tokens.shape
-    row_total = window_count * span_rows
-    head_size = model_width // HEADS
-    head_shape = (row_total // BLOCK, BLOCK, HEADS, head_size)
-    keep_rows = valid_mask.reshape(row_total, 1).astype(jnp.float32)
-    hidden = tokens.reshape(row_total, model_width).astype(jnp.float32) + condition.reshape(
-        row_total, model_width
-    ).astype(jnp.float32)
-    full_qkv, full_out, full_fc, full_down, full_gains, full_biases, full_fc_bias = gather_all(
-        w_qkv, w_out, w_fc, w_down, norm_gains, biases, fc_bias
-    )
-    gain_f = full_gains.astype(jnp.float32)
-    bias_f = full_biases.astype(jnp.float32)
-    normed_f, norm_back_one = jax.vjp(layer_norm, hidden, gain_f[0], bias_f[0])
-    normed = normed_f.astype(jnp.bfloat16)
-    projected = jnp.dot(normed, full_qkv, preferred_element_type=jnp.float32)
-    queries = (projected[:, :model_width] + bias_f[1]).astype(jnp.bfloat16).reshape(head_shape)
-    key_rows = projected[:, model_width : 2 * model_width].astype(jnp.bfloat16).reshape(head_shape)
-    values = (projected[:, 2 * model_width :] + bias_f[2]).astype(jnp.bfloat16).reshape(head_shape)
-    scores = masked_scores(queries, key_rows)
-    row_max = jnp.max(scores, axis=-1, keepdims=True)
-    log_total = row_max + jnp.log(jnp.sum(jnp.exp(scores - row_max), axis=-1, keepdims=True))
-    probs = jnp.exp(scores - log_total).astype(jnp.bfloat16)
-    mixed = jnp.einsum("bhqk,bkhd->bqhd", probs, values, preferred_element_type=jnp.float32)
-    mixed = mixed.reshape(row_total, model_width).astype(jnp.bfloat16)
-    after_attn = hidden + jnp.dot(mixed, full_out, preferred_element_type=jnp.float32) + bias_f[3]
-    vecs = jnp.concatenate([gain_f, bias_f], axis=0)
-    output, grad_after, grad_down_local, grad_w_fc, two_sums, grad_fc_bias_local = mlp(
-        True,
-        after_attn,
-        cotangent.reshape(row_total, model_width),
-        keep_rows,
+    tok, cond, cot = (a.reshape(D, D) for a in (tokens, condition, cotangent))
+    keep_rows = valid_mask.reshape(D, 1).astype(jnp.float32)
+    shards = (own_small(norm_gains, biases, fc_bias), w_qkv, w_out, w_fc, w_down)
+    _, full_qkv, full_out, full_fc, full_down, qkv, mixed, after, vecs, full_fc_bias = gather_and_attend(
+        shards, tok, cond
+    )
+    output, grad_after, grad_down_local, grad_w_fc, two_sums, fc_bias_sums = mlp(
+        True, after, cot, keep_rows, vecs, full_fc_bias, full_fc.reshape(D, FF), full_down.reshape(FF, D)
+    )
+    grad_input, grad_w_qkv, grad_w_out, grad_w_down, small = backward(
+        grad_after,
+        qkv,
+        mixed,
+        tok,
+        cond,
+        full_qkv.reshape(D, 3 * D),
+        full_out.reshape(D, D),
+        grad_down_local.reshape(2, 2, 4, 2, 128, D),
         vecs,
-        full_fc_bias.astype(jnp.float32).reshape(1, -1),
-        full_fc,
-        full_down,
-    )
-    output = output.reshape(tokens.shape)
-    grad_fc_bias_local = grad_fc_bias_local.reshape(-1)
-    back_qkv, back_out = full_qkv, full_out
-    grad_attn = grad_after.astype(jnp.bfloat16)
-    grad_out_local = outer_sum(mixed, grad_attn)
-    grad_mixed = times_transposed(grad_attn, back_out).astype(jnp.bfloat16).reshape(head_shape)
-    probs_full = jnp.exp(masked_scores(queries, key_rows) - log_total)
-    grad_probs = jnp.einsum(
-        "bqhd,bkhd->bhqk", grad_mixed, values, preferred_element_type=jnp.float32
-    )
-    grad_values = jnp.einsum(
-        "bhqk,bqhd->bkhd", probs, grad_mixed, preferred_element_type=jnp.float32
-    )
-    grad_values = grad_values.reshape(row_total, model_width).astype(jnp.bfloat16)
-    grad_scores = probs_full * (
-        grad_probs - jnp.sum(probs_full * grad_probs, axis=-1, keepdims=True)
-    )
-    grad_scores = grad_scores.astype(jnp.bfloat16)
-    grad_queries = (
-        jnp.einsum("bhqk,bkhd->bqhd", grad_scores, key_rows, preferred_element_type=jnp.float32)
-        * 0.125
-    )
-    grad_keys = (
-        jnp.einsum("bhqk,bqhd->bkhd", grad_scores, queries, preferred_element_type=jnp.float32)
-        * 0.125
-    )
-    grad_queries = grad_queries.reshape(row_total, model_width).astype(jnp.bfloat16)
-    grad_keys = grad_keys.reshape(row_total, model_width).astype(jnp.bfloat16)
-    grad_query_bias = jnp.sum(grad_queries.astype(jnp.float32), axis=0)
-    grad_value_bias = jnp.sum(grad_values.astype(jnp.float32), axis=0)
-    grad_projected = jnp.concatenate([grad_queries, grad_keys, grad_values], axis=1)
-    grad_qkv_local = outer_sum(normed, grad_projected)
-    grad_normed = times_transposed(grad_projected, back_qkv)
-    grad_hidden_norm, grad_gain_one, grad_shift_one = norm_back_one(grad_normed)
-    grad_input = (grad_after + grad_hidden_norm).astype(jnp.bfloat16).reshape(tokens.shape)
-    gains_local = jnp.stack([grad_gain_one, two_sums[0]])
-    biases_local = jnp.stack(
-        [
-            grad_shift_one,
-            grad_query_bias,
-            grad_value_bias,
-            two_sums[3],
-            two_sums[1],
-            two_sums[2],
-        ]
-    )
-    grad_w_qkv, grad_w_out, grad_w_down, grad_gains, grad_biases, grad_fc_bias = scatter_all(
-        grad_qkv_local, grad_out_local, grad_down_local,
-        gains_local, biases_local, grad_fc_bias_local,
-    )
+        two_sums,
+        fc_bias_sums,
+    )
+    grad_gains, grad_biases, grad_fc_bias = own_sums(small)
     return (
-        output,
-        grad_input,
+        output.reshape(tokens.shape),
+        grad_input.reshape(tokens.shape),
         grad_w_qkv,
         grad_w_out,
         grad_w_fc,

time: 503 us -> 387 us (0.77)
  matrix products: 70.2 us -> 0 us
  local copies, waits for them, and re-layouts: 67.9 us -> 12 us
  Pallas kernels: 326 us -> 364 us
  other arithmetic: 31.8 us -> 2.72 us
    dot_general x12 -> x0, matrix products: 70.2 us -> none  [the longest x2 15.3 us: outer_sum(): lax.dot_general(first, second, (((0,), (0,)), ((), ())), preferred_elemen...]
    reshape x10 -> x0, local copies, waits for them, and re-layouts: 40.5 us -> none  [the longest x2 12.4 us: body(): times_transposed(grad_attn, back_out).astype(jnp.bfloat16)]
    pallas_call x2, Pallas kernels: 237 us -> 273 us  [the longest x1 148 us: gather_and_attend(): pl.pallas_call(gather_kernel, out_shape=[jax.ShapeDtypeStruct((2, 2, 4, 2...]
    convert_element_type x7 -> x0, other arithmetic: 18.5 us -> none  [the longest x1 6.07 us: body(): (projected[:, :model_width] + bias_f[1]).astype(jnp.bfloat16)]
    convert_element_type x8 -> x0, local copies, waits for them, and re-layouts: 10.1 us -> none  [the longest x1 3.12 us: body(): mixed = mixed.reshape(row_total, model_width).astype(jnp.bfloat16)]
    reduce_sum x4 -> x0, other arithmetic: 9.79 us -> none  [the longest x1 3.68 us: layer_norm(): centered = rows_in - row_mean]
where the time goes in v3:
time: 387 us; the launch traced here: 380 us
  Pallas kernels  364 us (94%)
  local copies, waits for them, and re-layouts  12 us (3%)
    pallas_call x1, Pallas kernels, gather_and_attend(): pl.pallas_call(gather_kernel, out_shape=[jax.ShapeDtypeStruct((2, 2, 4, 2...  148 us
    pallas_call x1, Pallas kernels, backward(): pl.pallas_call(backward_kernel, out_shape=[jax.ShapeDtypeStruct((D, D), b...  126 us
    pallas_call x1, Pallas kernels, mlp(): pl.pallas_call(functools.partial(mlp_kernel, comm), out_shape=[jax.ShapeD...  90.5 us
    unnamed x18, local copies, waits for them, and re-layouts  8.59 us

profile of v3, /device:TPU:0, one launch (start us, length us, event | category | flops | bytes accessed | tf_op | source)
XLA Modules:
  0.0 379.7 jit_solution(1348323243572749260)
XLA Ops:
  0.7 0.1 broadcast_in_dim.31
  0.7 0.1 broadcast_in_dim.32
  0.8 0.1 pad.2.clone
  0.9 0.7 pad_maximum_fusion
  1.6 0.7 convert_bitcast_fusion
  2.3 0.1 broadcast_in_dim.35
  2.4 1.3 maximum_maximum_fusion.small
  3.7 1.0 copy.22
  4.8 147.7 %shard_map.178 = (bf16[2,2,4,2,16,128]{5,4,3,2,1,0:T(8,128)(2,1)}, bf16[2,2,4,2,32,3072]{5,4,3,2,1,0:T(8,128)(2,1)}, bf16[2,2,4,2,32,1024]{5,4,3,2,1,0:T(8,128)(...) custom-call(bf16[16,128]{1,0:T(8,128)(2,1)} %maximum_maximum_fusion., ...), custom_call_target="tpu_custom_call" | custom-call | tf_op jit(solution)/shard_map/pallas_call | solution.py:623
  152.5 90.5 %shard_map.179 = (bf16[1024,1024]{1,0:T(8,128)(2,1)}, f32[1024,1024]{1,0:T(8,128)}, bf16[4096,1024]{1,0:T(8,128)(2,1)}, f32[32,4096]{1,0:T(8,128)}, f32[8,1024]{1,0:T(8,128)}, /*index=5*/f32[1,4096]{1,0:T(1,128)}) custom-call(f32[1024,1024]{1,0:T(8,128)} %get-tuple-element.29.after_hbm, bf16[1024,1024]{1,0:T(8,128)(2,1)} %bitcast.26, f32[1024,1]{1,0:T(8,128)} %bitcast.27, ...), custom_call_target="tpu_custom_call" | custom-call | tf_op jit(solution)/shard_map/pallas_call | solution.py:421
  243.0 125.5 %shard_map.180 = (bf16[1024,1024]{1,0:T(8,128)(2,1)}, f32[32,3072]{1,0:T(8,128)}, f32[32,1024]{1,0:T(8,128)}, f32[128,1024]{1,0:T(8,128)}, f32[16,128]{1,0:T(8,128)}) custom-call(f32[1024,1024]{1,0:T(8,128)} %get-tuple-element.35.gafter_hbm, bf16[1024,3072]{1,0:T(8,128)(2,1)} %get-tuple-element.36.qkv_hbm, bf16[1024,1024]{1,0:T(8,128)(2,1)} %get-tuple-element.37.mixed_hbm, ...), custom_call_target="tpu_custom_call" | custom-call | tf_op jit(solution)/shard_map/pallas_call | solution.py:812
  368.6 1.2 slice_bitcast_fusion
  369.8 0.7 constant_dynamic-slice_fusion
  370.5 0.6 slice.9
  371.1 0.6 slice.10
  371.7 3.2 copy.29
  374.9 0.0 copy-done
  374.9 1.3 copy.30
  376.2 0.7 copy.31
  377.0 0.0 copy-done.4
  377.0 0.7 copy.32
  377.6 0.0 copy-done.1
  377.6 0.8 copy.33
  378.4 0.8 copy.34
  (12 shorter events, 0.0 us)
Async XLA Ops:
  371.7 3.2 copy-start
  374.9 1.3 copy-start.3
  374.9 2.1 copy-start.4
  374.9 2.7 copy-start.1
  376.2 2.2 copy-start.2
